TPU v7x, 256 devices: a whole 4x4x8 slice. The times are simulated.
256 devices in a mesh: jgrp: 16 (over y, x), energy: 16 (over z, core).
Axes of the slice: x: 4, y: 4, z: 8, core: 2. Of those that a mesh axis runs over, the one named last changes fastest.
Arguments:
- s_real: bfloat16 [32, 256, 256, 256], P('jgrp', 'energy'), may hold values from -3 to 3
- s_imag: bfloat16 [32, 256, 256, 256], P('jgrp', 'energy'), may hold values from -3 to 3
- level_map: int32 [32, 256], P('jgrp'), may hold values from 0 to 511
- channel_count: int32 [32], P('jgrp'), may hold values from 1 to 256, as said below
- prefactor: float32 [512, 256], P(None, 'energy'), may hold values from 0.003 to 0.03
- maxwell: float32 [8, 256], P(None, 'energy'), may hold values from 0.000390625 to 0.00390625
Outputs:
- rates: float32 [512, 8, 512], P(('jgrp', 'energy'))
Inputs may be any that keep to these rules, and one draw needn't show every extreme that they name: `channel_count`: rises with J from about 256 / 4; the last block has exactly 256.
All inputs are finite; a program needn't handle non-finite values.
Results may differ from a plain program's by a relative error of at most 0.0003.
Values sent between devices are 32-bit elements; how exact they have to be, the bound alone decides.
No kernel may reach another device: no remote copies, remote signals or barrier semaphores. Data moves between devices by JAX's collectives and lax.ppermute only.
A program may use at most 128 MiB of HBM per device.

v0:
```python
import functools

import jax
import jax.numpy as jnp
from jax import lax
from jax.experimental import pallas as pl
from jax.experimental.pallas import tpu as pltpu
from jax.sharding import Mesh, PartitionSpec as P

PLAN = (((0, 4), (4, 16)), ((0, 16),))
GROUP = 16
LANES = 128
EARLY = 3


def split2(x):
    hi = x.astype(jnp.bfloat16)
    lo = (x - hi.astype(jnp.float32)).astype(jnp.bfloat16)
    return hi, lo


def split3(x):
    hi, mid = split2(x)
    lo = (x - hi.astype(jnp.float32) - mid.astype(jnp.float32)).astype(jnp.bfloat16)
    return hi, mid, lo


def iota(shape, axis):
    return lax.broadcasted_iota(jnp.int32, shape, axis)


def across(x, lanes):
    return jnp.concatenate([x] * (lanes // LANES), axis=1)


def order(z, core):
    sign = 1 - 2 * core
    return [z + sign * 2, z + sign, z - sign * 2, z - sign, z, z + sign * 3, z - sign * 3, z + 4]


def mix(rows_ref, scale_ref, weight, block, at):
    energies, chans = rows_ref.shape[1], rows_ref.shape[3]
    part = rows_ref[block, :, at, :].reshape(energies * GROUP, chans)
    temps = weight.shape[0] // GROUP
    hi, lo = split2(weight * jnp.concatenate([scale_ref[block, at, :]] * temps, axis=0))
    both = jnp.dot(jnp.concatenate([hi, lo], axis=0), part, preferred_element_type=jnp.float32)
    return (both[:temps * GROUP] + both[temps * GROUP:]).reshape(temps, GROUP, chans)


def groups(chans, core):
    half = chans // 2
    for mine in (False, True):
        base = (core if mine else 1 - core) * half
        for low in range(0, half, GROUP):
            yield mine, low, pl.ds(pl.multiple_of(base + low, GROUP), GROUP)


def rows_kernel(count_hbm, level_hbm, real_hbm, imag_hbm, pre_hbm, max_hbm,
                whole_ref, send_ref, keep_ref, send_0, send_1, keep_0, keep_1, rows_ref, scale_ref, weight_ref,
                real_ref, imag_ref, count_ref, level_ref, pre_ref, max_ref,
                same_ref, wide_ref, part_sem, small_sem):
    temps, energies = max_ref.shape
    levels = pre_ref.shape[1]
    blocks, chans = level_ref.shape
    half = chans // 2
    width = energies * GROUP
    smalls = []
    for i, pair in enumerate(((count_hbm, count_ref), (level_hbm, level_ref),
                              (pre_hbm, pre_ref), (max_hbm, max_ref))):
        smalls.append(pltpu.make_async_copy(*pair, small_sem.at[i]))
        smalls[-1].start()
    parts = [[] for _ in range(blocks)]
    for block in range(blocks):
        for step, (low, high) in enumerate(PLAN[block]):
            at = pl.ds(low, high - low)
            parts[block].append([
                pltpu.make_async_copy(x_hbm.at[block, at], x_ref.at[block, at], part_sem.at[i, block, step])
                for i, (x_hbm, x_ref) in enumerate(((real_hbm, real_ref), (imag_hbm, imag_ref)))
            ])
            for copy in parts[block][step]:
                copy.start()
    core = lax.axis_index("core")
    z = lax.axis_index("z")
    jgrp = lax.axis_index("y") * lax.axis_size("x") + lax.axis_index("x")
    delta = jnp.where(iota((LANES, LANES), 0) == iota((LANES, LANES), 1), 1.0, 0.0)
    turn = (((1,), (1,)), ((), ()))
    for copy in smalls[:2]:
        copy.wait()


    seg_cols = []
    for block in range(blocks):
        seg_row = jnp.where(iota((1, chans), 1) < count_ref[block], level_ref[pl.ds(block, 1), :], -1)
        seg_row = seg_row.astype(jnp.float32)
        seg_col = jnp.transpose(jnp.broadcast_to(seg_row, (LANES, chans)))
        same = across(seg_col, chans) == seg_row
        earlier = same & (iota((chans, chans), 1) < iota((chans, chans), 0))
        taken = jnp.dot(jnp.where(earlier, 1.0, 0.0).astype(jnp.bfloat16),
                        jnp.ones((chans, LANES), jnp.bfloat16), preferred_element_type=jnp.float32)
        lead = across(jnp.where((taken == 0.0) & (seg_col >= 0.0), 1.0, 0.0), chans)
        same_ref[block] = jnp.where(same, lead, 0.0).astype(jnp.bfloat16)
        seg_cols.append(seg_col)

    for block in range(blocks):
        factor = (2 * (jgrp * blocks + block) + 1).astype(jnp.float32)
        for step, (low, high) in enumerate(PLAN[block]):
            for copy in parts[block][step]:
                copy.wait()
            for e in range(low, high):
                real = real_ref[block, e].astype(jnp.float32)
                imag = imag_ref[block, e].astype(jnp.float32)
                on = [delta - real[k:k + LANES, k:k + LANES] for k in range(0, chans, LANES)]
                real = jnp.concatenate([
                    jnp.concatenate([on[0], real[:LANES, LANES:]], axis=1),
                    jnp.concatenate([real[LANES:, :LANES], on[1]], axis=1)], axis=0)
                weighted = ((real ** 2 + imag ** 2) * factor).astype(jnp.bfloat16)
                rowsum = jnp.dot(same_ref[block], weighted, preferred_element_type=jnp.float32)
                rows_ref[block, e] = rowsum.astype(jnp.bfloat16)
        if block == 0:
            for copy in smalls[2:]:
                copy.wait()
            spread = iota((3 * energies, width), 1) // GROUP == iota((3 * energies, width), 0) % energies
            spread = jnp.where(spread, 1.0, 0.0).astype(jnp.bfloat16)
            wide_ref[...] = jnp.dot(jnp.concatenate(split3(max_ref[...]), axis=1), spread,
                                    preferred_element_type=jnp.float32)
            hit = iota((GROUP, width), 1) % GROUP == iota((GROUP, width), 0)
            for s, t in enumerate(order(z, core)):
                t = lax.rem(t + temps, temps)
                weight_ref[s * GROUP:(s + 1) * GROUP, :] = jnp.where(hit, wide_ref[pl.ds(t, 1), :], 0.0)
            pre = jnp.concatenate(split3(pre_ref[...]), axis=0)
        picks = across(seg_cols[block], levels) == iota((chans, levels), 1).astype(jnp.float32)
        picks = jnp.where(picks, 1.0, 0.0).astype(jnp.bfloat16)
        own = lax.dot_general(picks, pre, turn, preferred_element_type=jnp.float32)
        scale_ref[block] = jnp.dot(own.astype(jnp.bfloat16), spread, preferred_element_type=jnp.float32)
        weight = weight_ref[(temps - EARLY) * GROUP:, :]
        send_next, keep_next = ((send_0, keep_0), (send_1, keep_1))[block]
        for mine, low, at in groups(chans, core):
            total = mix(rows_ref, scale_ref, weight, block, at)
            front, back = (low, half + low) if mine else (half + low, low)
            keep_next[front:front + GROUP, :] = total[0]
            send_next[back:back + GROUP, :] = total[1]
            if block == 0:
                whole_ref[front:front + GROUP, :] = total[2]
            else:
                (keep_ref if mine else send_ref)[low:low + GROUP, :] = total[2]


def rest_kernel(count_ref, level_ref, rows_ref, scale_ref, weight_ref, *refs):
    picks_ref, columns_ref = refs[-2:]
    blocks, _, chans, _ = rows_ref.shape
    half = chans // 2
    core = lax.axis_index("core")
    weight = weight_ref[:weight_ref.shape[0] - EARLY * GROUP, :]
    for block in range(blocks):
        send_ref, keep_ref = refs[block], refs[blocks + block]
        for mine, low, at in groups(chans, core):
            total = mix(rows_ref, scale_ref, weight, block, at)
            front, back = (low, half + low) if mine else (half + low, low)
            for k in range(2):
                keep_ref[k * chans + front:k * chans + front + GROUP, :] = total[k]
                send_ref[k * chans + back:k * chans + back + GROUP, :] = total[2 + k]
            (keep_ref if mine else send_ref)[2 * chans + low:2 * chans + low + GROUP, :] = total[4]

    levels = columns_ref.shape[1]
    row = iota((levels // 2, chans), 0)
    wanted = row // 2 * 4 + core * 2 + row % 2
    for block in range(blocks):
        seg = jnp.where(iota((1, chans), 1) < count_ref[block], level_ref[pl.ds(block, 1), :], -1)
        columns_ref[block] = jnp.where(iota((levels, chans), 0) == seg, 1.0, 0.0).astype(jnp.bfloat16)
        turned = jnp.concatenate([seg[:, half:], seg[:, :half]], axis=1)
        seg = jnp.where(core == 0, seg, turned)
        picks_ref[block] = jnp.where(wanted == seg, 1.0, 0.0).astype(jnp.bfloat16)


def rows(counts, level_map, s_real, s_imag, prefactor, maxwell):
    blocks, energies, chans = s_real.shape[:3]
    temps = maxwell.shape[0]
    width = energies * GROUP
    first = jax.ShapeDtypeStruct((chans // 2, chans), jnp.float32)
    second = jax.ShapeDtypeStruct((chans, chans), jnp.float32)
    hbm = pl.BlockSpec(memory_space=pltpu.HBM)
    vmem = pl.BlockSpec(memory_space=pltpu.VMEM)
    args = (counts, level_map, s_real, s_imag, prefactor, maxwell)
    return pl.pallas_call(
        rows_kernel,
        out_shape=[second] + [first] * 2 + [second] * (2 * blocks) + [
                   jax.ShapeDtypeStruct(s_real.shape, jnp.bfloat16),
                   jax.ShapeDtypeStruct((blocks, chans, width), jnp.float32),
                   jax.ShapeDtypeStruct((temps * GROUP, width), jnp.float32)],
        in_specs=[hbm] * 6,
        out_specs=[vmem] * (6 + 2 * blocks),
        scratch_shapes=[
            pltpu.VMEM(s_real.shape, jnp.bfloat16),
            pltpu.VMEM(s_imag.shape, jnp.bfloat16),
            pltpu.SMEM(counts.shape, jnp.int32),
            pltpu.VMEM(level_map.shape, jnp.int32),
            pltpu.VMEM(prefactor.shape, jnp.float32),
            pltpu.VMEM(maxwell.shape, jnp.float32),
            pltpu.VMEM((blocks, chans, chans), jnp.bfloat16),
            pltpu.VMEM((temps, width), jnp.float32),
            pltpu.SemaphoreType.DMA((2, blocks, len(PLAN[0]))),
            pltpu.SemaphoreType.DMA((4,)),
        ],
        compiler_params=pltpu.CompilerParams(vmem_limit_bytes=24 * 2**20),
        name="rows",
    )(*[pltpu.with_memory_space_constraint(x, pltpu.HBM) for x in args])


def rest(counts, level_map, levels, rows, scale, weight):
    blocks, _, chans, _ = rows.shape
    out = jax.ShapeDtypeStruct((2 * chans + chans // 2, chans), jnp.float32)
    vmem = pl.BlockSpec(memory_space=pltpu.VMEM)
    *out, picks, columns = pl.pallas_call(
        rest_kernel,
        out_shape=[out] * (2 * blocks) + [jax.ShapeDtypeStruct((blocks, levels // 2, chans), jnp.bfloat16),
                                          jax.ShapeDtypeStruct((blocks, levels, chans), jnp.bfloat16)],
        in_specs=[pl.BlockSpec(memory_space=pltpu.SMEM)] + [vmem] * 4,
        out_specs=[vmem] * (2 * blocks + 2),
        compiler_params=pltpu.CompilerParams(vmem_limit_bytes=24 * 2**20),
        name="rest",
    )(counts, level_map, rows, scale, weight)
    return out[:blocks], out[blocks:], picks, columns


def spread_kernel(picks_ref, columns_ref, *refs):
    turn = (((1,), (1,)), ((), ()))
    blocks, _, chans = picks_ref.shape
    half = chans // 2
    total = None
    for block in range(blocks):
        other = refs[blocks + block]
        both = refs[block][...] + jnp.concatenate([other[half:], other[:half]], axis=0)
        hi, lo = split2(both)
        wide = lax.dot_general(jnp.concatenate([hi, lo], axis=0), columns_ref[block], turn,
                               preferred_element_type=jnp.float32)
        hi, lo = split2(wide[:chans] + wide[chans:])
        term = jnp.dot(picks_ref[block], hi, preferred_element_type=jnp.float32)
        term += jnp.dot(picks_ref[block], lo, preferred_element_type=jnp.float32)
        total = term if total is None else total + term
    refs[-1][...] = total


def spread(picks, columns, *parts):
    whole = pl.BlockSpec(memory_space=pltpu.VMEM)
    return pl.pallas_call(
        spread_kernel,
        out_shape=jax.ShapeDtypeStruct((picks.shape[1], columns.shape[1]), jnp.float32),
        in_specs=[whole] * (2 + len(parts)),
        out_specs=whole,
        compiler_params=pltpu.CompilerParams(vmem_limit_bytes=16 * 2**20),
        name="spread",
    )(picks, columns, *parts)


def body(s_real, s_imag, level_map, channel_count, prefactor, maxwell):
    blocks, _, chans = s_real.shape[:3]
    levels = prefactor.shape[0]
    half = chans // 2
    n = lax.axis_size("z")
    swap = [(0, 1), (1, 0)]
    ring = [(2 * i, (i + 1) % n * 2) for i in range(n)]
    ring += [(2 * i + 1, (i - 1) % n * 2 + 1) for i in range(n)]

    def move(x):
        return lax.ppermute(x, ("z", "core"), ring)

    whole, send, keep, *held = rows(channel_count, level_map, s_real, s_imag, prefactor.T, maxwell)
    send_next, keep_next, held = held[:blocks], held[blocks:2 * blocks], held[2 * blocks:]
    other = lax.ppermute(send, "core", swap)
    send_next, other = lax.optimization_barrier((send_next, other))
    nexts = [x + lax.ppermute(y, "core", swap) for x, y in zip(keep_next, send_next)]
    held[0], first = lax.optimization_barrier((held[0], keep + other))
    carries = [move(whole), move(first)]
    send_rest, keep_rest, picks, columns = rest(channel_count, level_map, levels, *held)
    carries[0], send_rest = lax.optimization_barrier((carries[0], send_rest))
    others_rest = [lax.ppermute(x, "core", swap) for x in send_rest]
    mine = []
    for block, carry in enumerate(carries):
        if block == 0:
            carry = nexts[block] + carry
        else:
            carry = jnp.concatenate([nexts[block][:half] + carry, nexts[block][half:]])
        other_rest = others_rest[block]

        def own(low, high):
            return keep_rest[block][low:high] + other_rest[low:high]

        carry = move(carry)
        for k in range(2):
            carry = move(own(k * chans, (k + 1) * chans) + carry)
        mine.append(jnp.concatenate([own(2 * chans, 2 * chans + half) + carry[:half], carry[half:]]))
    others = [lax.ppermute(x, "core", swap) for x in mine]
    part = spread(picks, columns, *mine, *others)
    size = lax.axis_size("y") * lax.axis_size("x")
    part = part.reshape(size, levels // 2 // size, levels)
    part = lax.all_to_all(part, ("y", "x"), 0, 0, tiled=True).sum(0)
    part = lax.all_to_all(part.reshape(n, part.shape[0] // n, levels), "z", 0, 0, tiled=True)
    return jnp.transpose(part, (1, 0, 2))


def solution(mesh):
    fine = Mesh(mesh.devices.reshape(4, 4, 8, 2), ("y", "x", "z", "core"))
    jgrp, energy = ("y", "x"), ("z", "core")
    in_specs = (
        P(jgrp, energy, None, None),
        P(jgrp, energy, None, None),
        P(jgrp, None),
        P(jgrp),
        P(None, energy),
        P(None, energy),
    )
    out_specs = P(("y", "x", "z", "core"), None, None)
    return jax.shard_map(body, mesh=fine, in_specs=in_specs, out_specs=out_specs, check_vma=False)
```

profile of v0, /device:TPU:2, one launch (start us, length us, event | category | flops | bytes accessed | tf_op | source)
XLA Modules:
  0.0 80.0 jit_solution(15958225460647857936)
XLA Ops:
  0.0 7.2 %rows.1 = (f32[256,256]{1,0:T(8,128)S(1)}, f32[128,256]{1,0:T(8,128)S(1)}, f32[128,256]{1,0:T(8,128)S(1)}, f32[256,256]{1,0:T(8,128)S(1)}, f32[256,256]{1,0:T(8,...) custom-call(s32[2]{0:T(128)} %count_ref.1, ...), custom_call_target="tpu_custom_call" | custom-call | tf_op jit(solution)/shard_map/rows/pallas_call | solution.py:184
  7.2 0.1 collective-permute-start
  7.3 2.0 %collective-permute-start.1 = (f32[256,256]{1,0:T(8,128)S(1)}, f32[256,256]{1,0:T(8,128)S(1)}, u32[]{:S(2)}, u32[]{:S(2)}) collective-permute-start(f32[256,256]{1,0:T(8,128)S(1)} %get-tuple-element.41), channel_id=1, source_target_pairs={{0,2},{2,4},{4,6},{6,8},{8,10},{10,12},{12,14},{14,0},{1,15},{3,1}... | collective-permute-start | bytes 786440 | tf_op jit(solution)/shard_map/ppermute | solution.py:265
  9.3 4.1 %collective-permute-start.8 = (f32[256,256]{1,0:T(8,128)S(1)}, f32[256,256]{1,0:T(8,128)S(1)}, u32[]{:S(2)}, u32[]{:S(2)}) collective-permute-start(f32[256,256]{1,0:T(8,128)S(1)} %get-tuple-element.51), channel_id=1, source_target_pairs={{0,1},{1,0},{2,3},{3,2},{4,5},{5,4},{6,7},{7,6},{8,9},{9,8},{10,11... | collective-permute-start | bytes 786440 | tf_op jit(solution)/shard_map/ppermute | solution.py:271
  13.4 0.1 collective-permute-start.9
  13.5 1.7 %rest.1 = (f32[640,256]{1,0:T(8,128)S(1)}, f32[640,256]{1,0:T(8,128)S(1)}, f32[640,256]{1,0:T(8,128)S(1)}, f32[640,256]{1,0:T(8,128)S(1)}, bf16[2,256,256]{2,1,0...) custom-call(s32[2]{0:T(128)S(1)} %copy-done.1, s32[2,256]{1,0:T(2,128)S(1)} %copy-done, ...), custom_call_target="tpu_custom_call" | custom-call | tf_op jit(solution)/shard_map/rest/pallas_call | solution.py:213
  15.2 2.4 %collective-permute-done.1 = f32[256,256]{1,0:T(8,128)S(1)} collective-permute-done((f32[256,256]{1,0:T(8,128)S(1)}, f32[256,256]{1,0:T(8,128)S(1)}, u32[]{:S(2)}, u32[]{:S(2)}) %collective-permute-start.1) | collective-permute-done | bytes 262176 | tf_op jit(solution)/shard_map/ppermute | solution.py:265
  17.6 0.5 collective-permute-start.3
  18.2 1.5 %collective-permute-done.9 = f32[128,256]{1,0:T(8,128)S(1)} collective-permute-done((f32[128,256]{1,0:T(8,128)S(1)}, f32[128,256]{1,0:T(8,128)S(1)}, u32[]{:S(2)}, u32[]{:S(2)}) %collective-permute-start.9) | collective-permute-done | bytes 131104 | tf_op jit(solution)/shard_map/ppermute | solution.py:265
  19.7 0.1 collective-permute-start.10
  19.8 0.3 collective-permute-done.3
  20.1 0.1 add_add_fusion
  20.1 0.1 collective-permute-start.4
  20.2 7.2 %collective-permute-done.10 = f32[256,256]{1,0:T(8,128)S(1)} collective-permute-done((f32[256,256]{1,0:T(8,128)S(1)}, f32[256,256]{1,0:T(8,128)S(1)}, u32[]{:S(2)}, u32[]{:S(2)}) %collective-permute-start.10) | collective-permute-done | bytes 262176 | tf_op jit(solution)/shard_map/ppermute | solution.py:265
  27.4 0.1 fusion
  27.5 0.1 collective-permute-start.11
  27.5 2.6 %collective-permute-done.4 = f32[256,256]{1,0:T(8,128)S(1)} collective-permute-done((f32[256,256]{1,0:T(8,128)S(1)}, f32[256,256]{1,0:T(8,128)S(1)}, u32[]{:S(2)}, u32[]{:S(2)}) %collective-permute-start.4) | collective-permute-done | bytes 262176 | tf_op jit(solution)/shard_map/ppermute | solution.py:265
  30.2 0.1 fusion.2
  30.3 0.3 collective-permute-start.5
  30.5 4.6 %collective-permute-done.11 = f32[256,256]{1,0:T(8,128)S(1)} collective-permute-done((f32[256,256]{1,0:T(8,128)S(1)}, f32[256,256]{1,0:T(8,128)S(1)}, u32[]{:S(2)}, u32[]{:S(2)}) %collective-permute-start.11) | collective-permute-done | bytes 262176 | tf_op jit(solution)/shard_map/ppermute | solution.py:265
  35.2 0.1 collective-permute-start.12
  35.3 2.8 %collective-permute-done.5 = f32[256,256]{1,0:T(8,128)S(1)} collective-permute-done((f32[256,256]{1,0:T(8,128)S(1)}, f32[256,256]{1,0:T(8,128)S(1)}, u32[]{:S(2)}, u32[]{:S(2)}) %collective-permute-start.5) | collective-permute-done | bytes 262176 | tf_op jit(solution)/shard_map/ppermute | solution.py:265
  38.2 0.1 collective-permute-start.6
  38.3 4.6 %collective-permute-done.12 = f32[256,256]{1,0:T(8,128)S(1)} collective-permute-done((f32[256,256]{1,0:T(8,128)S(1)}, f32[256,256]{1,0:T(8,128)S(1)}, u32[]{:S(2)}, u32[]{:S(2)}) %collective-permute-start.12) | collective-permute-done | bytes 262176 | tf_op jit(solution)/shard_map/ppermute | solution.py:265
  42.9 0.1 collective-permute-start.14
  43.0 2.8 %collective-permute-done.6 = f32[256,256]{1,0:T(8,128)S(1)} collective-permute-done((f32[256,256]{1,0:T(8,128)S(1)}, f32[256,256]{1,0:T(8,128)S(1)}, u32[]{:S(2)}, u32[]{:S(2)}) %collective-permute-start.6) | collective-permute-done | bytes 262176 | tf_op jit(solution)/shard_map/ppermute | solution.py:265
  45.9 0.1 collective-permute-start.13
  46.0 1.5 %collective-permute-done.13.refs_2_ = f32[256,256]{1,0:T(8,128)S(1)} collective-permute-done((f32[256,256]{1,0:T(8,128)S(1)}, f32[256,256]{1,0:T(8,128)S(1)}, u32[]{:S(2)}, u32[]{:S(2)}) %collective-permute-start.13) | collective-permute-done | bytes 262176 | tf_op jit(solution)/shard_map/ppermute | solution.py:292
  47.5 1.0 %spread.1 = f32[256,512]{1,0:T(8,128)S(1)} custom-call(bf16[2,256,256]{2,1,0:T(8,128)(2,1)S(1)} %get-tuple-element.38.picks_ref, bf16[2,512,256]{2,1,0:T(8,128)(2,1)S(1)} %get-tuple-element.39.columns_ref, f32[256,256]{1,0:T(8,128)S(1)} %pad_maximum_fusion.refs_0_, f32[256,256]{1,0:T(8,128)S(1)} %pad_maximum_fusion.2.refs_1_, ...), custom_call_target="tpu_custom_call" | custom-call | tf_op jit(solution)/shard_map/spread/pallas_call | solution.py:245
  48.6 17.7 %all_to_all.10 = f32[16,16,512]{2,1,0:T(8,128)S(1)} all-to-all(f32[16,16,512]{2,1,0:T(8,128)S(1)} %bitcast.3), channel_id=1, replica_groups=mesh['y'=4,'x'=4,'z'=8,'core'=2] {'y','x'}, dimensions={0} | all-to-all | bytes 1048576 | tf_op jit(solution)/shard_map/all_to_all | solution.py:296
  66.4 13.0 %all_to_all.11 = f32[8,2,512]{2,1,0:T(2,128)S(1)} all-to-all(f32[8,2,512]{2,1,0:T(2,128)S(1)} %reshape.7), channel_id=1, replica_groups=mesh['y'=4,'x'=4,'z'=8,'core'=2] {'z'}, dimensions={0} | all-to-all | bytes 65536 | tf_op jit(solution)/shard_map/all_to_all | solution.py:297
  79.4 0.6 copy.7
  (23 shorter events, 0.4 us)
Async XLA Ops:
  0.0 13.5 %copy-start = (s32[2,256]{1,0:T(2,128)S(1)}, s32[2,256]{1,0:T(2,128)}, u32[]{:S(2)}) copy-start(s32[2,256]{1,0:T(2,128)} %level_ref.1) | copy-start | bytes 6148
  0.0 13.5 %copy-start.1 = (s32[2]{0:T(128)S(1)}, s32[2]{0:T(128)}, u32[]{:S(2)}) copy-start(s32[2]{0:T(128)} %count_ref.1) | copy-start | bytes 28
  7.2 2.1 %collective-permute-start = (f32[128,256]{1,0:T(8,128)S(1)}, f32[128,256]{1,0:T(8,128)S(1)}, u32[]{:S(2)}, u32[]{:S(2)}) collective-permute-start(f32[128,256]{1,0:T(8,128)S(1)} %get-tuple-element.33), channel_id=1, source_target_pairs={{0,1},{1,0},{2,3},{3,2},{4,5},{5,4},{6,7},{7,6},{8,9},{9,8},{10,11... | collective-permute-start | bytes 393224 | tf_op jit(solution)/shard_map/ppermute | solution.py:269
  7.3 10.3 %collective-permute-start.1 = (f32[256,256]{1,0:T(8,128)S(1)}, f32[256,256]{1,0:T(8,128)S(1)}, u32[]{:S(2)}, u32[]{:S(2)}) collective-permute-start(f32[256,256]{1,0:T(8,128)S(1)} %get-tuple-element.41), channel_id=1, source_target_pairs={{0,2},{2,4},{4,6},{6,8},{8,10},{10,12},{12,14},{14,0},{1,15},{3,1}... | collective-permute-start | bytes 786440 | tf_op jit(solution)/shard_map/ppermute | solution.py:265
  9.3 8.8 %collective-permute-start.8 = (f32[256,256]{1,0:T(8,128)S(1)}, f32[256,256]{1,0:T(8,128)S(1)}, u32[]{:S(2)}, u32[]{:S(2)}) collective-permute-start(f32[256,256]{1,0:T(8,128)S(1)} %get-tuple-element.51), channel_id=1, source_target_pairs={{0,1},{1,0},{2,3},{3,2},{4,5},{5,4},{6,7},{7,6},{8,9},{9,8},{10,11... | collective-permute-start | bytes 786440 | tf_op jit(solution)/shard_map/ppermute | solution.py:271
  13.4 6.3 %collective-permute-start.9 = (f32[128,256]{1,0:T(8,128)S(1)}, f32[128,256]{1,0:T(8,128)S(1)}, u32[]{:S(2)}, u32[]{:S(2)}) collective-permute-start(f32[128,256]{1,0:T(8,128)S(1)} %add.51), channel_id=1, source_target_pairs={{0,2},{2,4},{4,6},{6,8},{8,10},{10,12},{12,14},{14,0},{1,15},{3,1}... | collective-permute-start | bytes 393224 | tf_op jit(solution)/shard_map/ppermute | solution.py:265
  17.6 9.8 %collective-permute-start.7 = (f32[640,256]{1,0:T(8,128)S(1)}, f32[640,256]{1,0:T(8,128)S(1)}, u32[]{:S(2)}, u32[]{:S(2)}) collective-permute-start(f32[640,256]{1,0:T(8,128)S(1)} %get-tuple-element.49), channel_id=1, source_target_pairs={{0,1},{1,0},{2,3},{3,2},{4,5},{5,4},{6,7},{7,6},{8,9},{9,8},{10,11... | collective-permute-start | bytes 1966088 | tf_op jit(solution)/shard_map/ppermute | solution.py:276
  17.6 2.5 %collective-permute-start.3 = (f32[256,256]{1,0:T(8,128)S(1)}, f32[256,256]{1,0:T(8,128)S(1)}, u32[]{:S(2)}, u32[]{:S(2)}) collective-permute-start(f32[256,256]{1,0:T(8,128)S(1)} %get-tuple-element.46), channel_id=1, source_target_pairs={{0,1},{1,0},{2,3},{3,2},{4,5},{5,4},{6,7},{7,6},{8,9},{9,8},{10,11... | collective-permute-start | bytes 786440 | tf_op jit(solution)/shard_map/ppermute | solution.py:271
  18.1 12.1 %collective-permute-start.2 = (f32[640,256]{1,0:T(8,128)S(1)}, f32[640,256]{1,0:T(8,128)S(1)}, u32[]{:S(2)}, u32[]{:S(2)}) collective-permute-start(f32[640,256]{1,0:T(8,128)S(1)} %get-tuple-element.44), channel_id=1, source_target_pairs={{0,1},{1,0},{2,3},{3,2},{4,5},{5,4},{6,7},{7,6},{8,9},{9,8},{10,11... | collective-permute-start | bytes 1966088 | tf_op jit(solution)/shard_map/ppermute | solution.py:276
  19.7 7.7 %collective-permute-start.10 = (f32[256,256]{1,0:T(8,128)S(1)}, f32[256,256]{1,0:T(8,128)S(1)}, u32[]{:S(2)}, u32[]{:S(2)}) collective-permute-start(f32[256,256]{1,0:T(8,128)S(1)} %pad_maximum_fusion.1), channel_id=1, source_target_pairs={{0,2},{2,4},{4,6},{6,8},{8,10},{10,12},{12,14},{14,0},{1,15},{3,1}... | collective-permute-start | bytes 786440 | tf_op jit(solution)/shard_map/ppermute | solution.py:265
  20.1 10.1 %collective-permute-start.4 = (f32[256,256]{1,0:T(8,128)S(1)}, f32[256,256]{1,0:T(8,128)S(1)}, u32[]{:S(2)}, u32[]{:S(2)}) collective-permute-start(f32[256,256]{1,0:T(8,128)S(1)} %add_add_fusion), channel_id=1, source_target_pairs={{0,2},{2,4},{4,6},{6,8},{8,10},{10,12},{12,14},{14,0},{1,15},{3,1}... | collective-permute-start | bytes 786440 | tf_op jit(solution)/shard_map/ppermute | solution.py:265
  27.5 7.7 %collective-permute-start.11 = (f32[256,256]{1,0:T(8,128)S(1)}, f32[256,256]{1,0:T(8,128)S(1)}, u32[]{:S(2)}, u32[]{:S(2)}) collective-permute-start(f32[256,256]{1,0:T(8,128)S(1)} %fusion), channel_id=1, source_target_pairs={{0,2},{2,4},{4,6},{6,8},{8,10},{10,12},{12,14},{14,0},{1,15},{3,1}... | collective-permute-start | bytes 786440 | tf_op jit(solution)/shard_map/ppermute | solution.py:265
  30.3 7.8 %collective-permute-start.5 = (f32[256,256]{1,0:T(8,128)S(1)}, f32[256,256]{1,0:T(8,128)S(1)}, u32[]{:S(2)}, u32[]{:S(2)}) collective-permute-start(f32[256,256]{1,0:T(8,128)S(1)} %fusion.2), channel_id=1, source_target_pairs={{0,2},{2,4},{4,6},{6,8},{8,10},{10,12},{12,14},{14,0},{1,15},{3,1}... | collective-permute-start | bytes 786440 | tf_op jit(solution)/shard_map/ppermute | solution.py:265
  35.2 7.7 %collective-permute-start.12 = (f32[256,256]{1,0:T(8,128)S(1)}, f32[256,256]{1,0:T(8,128)S(1)}, u32[]{:S(2)}, u32[]{:S(2)}) collective-permute-start(f32[256,256]{1,0:T(8,128)S(1)} %fusion.1), channel_id=1, source_target_pairs={{0,2},{2,4},{4,6},{6,8},{8,10},{10,12},{12,14},{14,0},{1,15},{3,1}... | collective-permute-start | bytes 786440 | tf_op jit(solution)/shard_map/ppermute | solution.py:265
  38.2 7.7 %collective-permute-start.6 = (f32[256,256]{1,0:T(8,128)S(1)}, f32[256,256]{1,0:T(8,128)S(1)}, u32[]{:S(2)}, u32[]{:S(2)}) collective-permute-start(f32[256,256]{1,0:T(8,128)S(1)} %fusion.3), channel_id=1, source_target_pairs={{0,2},{2,4},{4,6},{6,8},{8,10},{10,12},{12,14},{14,0},{1,15},{3,1}... | collective-permute-start | bytes 786440 | tf_op jit(solution)/shard_map/ppermute | solution.py:265
  42.9 3.1 %collective-permute-start.14 = (f32[256,256]{1,0:T(8,128)S(1)}, f32[256,256]{1,0:T(8,128)S(1)}, u32[]{:S(2)}, u32[]{:S(2)}) collective-permute-start(f32[256,256]{1,0:T(8,128)S(1)} %pad_maximum_fusion.2.refs_1_), channel_id=1, source_target_pairs={{0,1},{1,0},{2,3},{3,2},{4,5},{5,4},{6,7},{7,6},{8,9},{9,8},{10,11... | collective-permute-start | bytes 786440 | tf_op jit(solution)/shard_map/ppermute | solution.py:292
  45.9 1.6 %collective-permute-start.13 = (f32[256,256]{1,0:T(8,128)S(1)}, f32[256,256]{1,0:T(8,128)S(1)}, u32[]{:S(2)}, u32[]{:S(2)}) collective-permute-start(f32[256,256]{1,0:T(8,128)S(1)} %pad_maximum_fusion.refs_0_), channel_id=1, source_target_pairs={{0,1},{1,0},{2,3},{3,2},{4,5},{5,4},{6,7},{7,6},{8,9},{9,8},{10,11... | collective-permute-start | bytes 786440 | tf_op jit(solution)/shard_map/ppermute | solution.py:292
where the time goes:
time: 80.1 us; the launch traced here: 80 us
  blocking collectives  30.8 us (38%)
  waiting for transfers between devices  30.3 us (38%)
  Pallas kernels  9.92 us (12%)
  starting transfers between devices  7.63 us (10%)
    ppermute x8, waiting for transfers between devices, move(): return lax.ppermute(x, ('z', 'core'), ring)  28.5 us
    all_to_all x1, blocking collectives, body(): part = lax.all_to_all(part, ('y', 'x'), 0, 0, tiled=True).sum(0)  17.7 us
    all_to_all x1, blocking collectives, body(): lax.all_to_all(part.reshape(n, part.shape[0] // n, levels), 'z', 0, 0, ti...  13 us
    pallas_call x1, Pallas kernels, rows(): pl.pallas_call(rows_kernel, out_shape=[second] + [first] * 2 + [second] *...  7.2 us
    ppermute x2, starting transfers between devices, body(): lax.ppermute(y, 'core', swap)  4.59 us
    ppermute x8, starting transfers between devices, move(): return lax.ppermute(x, ('z', 'core'), ring)  2.76 us
    pallas_call x1, Pallas kernels, rest(): pl.pallas_call(rest_kernel, out_shape=[out] * (2 * blocks) + [jax.ShapeDt...  1.7 us
  transfers between devices with their start and end apart: 15, of which 10 were waited for; matrix products, arithmetic and copies ran while one was open for 1% of the time, Pallas kernels for 2%

commit v1 on v0

v1 whole, which is shorter than its diff:
```python
import functools

import jax
import jax.numpy as jnp
from jax import lax
from jax.experimental import pallas as pl
from jax.experimental.pallas import tpu as pltpu
from jax.sharding import Mesh, PartitionSpec as P

PLAN = (((0, 4), (4, 16)), ((0, 16),))
GROUP = 16
LANES = 128


def split2(x):
    hi = x.astype(jnp.bfloat16)
    lo = (x - hi.astype(jnp.float32)).astype(jnp.bfloat16)
    return hi, lo


def split3(x):
    hi, mid = split2(x)
    lo = (x - hi.astype(jnp.float32) - mid.astype(jnp.float32)).astype(jnp.bfloat16)
    return hi, mid, lo


def iota(shape, axis):
    return lax.broadcasted_iota(jnp.int32, shape, axis)


def across(x, lanes):
    return jnp.concatenate([x] * (lanes // LANES), axis=1)


def order(z, core):
    sign = 1 - 2 * core
    return [z + sign, z + sign + 4, z - sign, z - sign + 4, z, z + 4, z + 2 * sign, z - 2 * sign]


def mix(rows_ref, scale_ref, weight, at):
    energies, _, chans = rows_ref.shape
    part = rows_ref[:, at, :].reshape(energies * GROUP, chans)
    temps = weight.shape[0] // GROUP
    hi, lo = split2(weight * jnp.concatenate([scale_ref[at, :]] * temps, axis=0))
    both = jnp.dot(jnp.concatenate([hi, lo], axis=0), part, preferred_element_type=jnp.float32)
    return (both[:temps * GROUP] + both[temps * GROUP:]).reshape(temps, GROUP, chans)


def groups(chans, core):
    half = chans // 2
    for mine in (False, True):
        base = (core if mine else 1 - core) * half
        for low in range(0, half, GROUP):
            at = pl.ds(pl.multiple_of(base + low, GROUP), GROUP)
            yield (low, half + low, at) if mine else (half + low, low, at)


def spread_lanes(energies):
    shape = (3 * energies, energies * GROUP)
    hit = iota(shape, 1) // GROUP == iota(shape, 0) % energies
    return jnp.where(hit, 1.0, 0.0).astype(jnp.bfloat16)


def leaders(block, count_ref, level_ref):
    chans = level_ref.shape[1]
    seg_row = jnp.where(iota((1, chans), 1) < count_ref[block], level_ref[pl.ds(block, 1), :], -1)
    seg_row = seg_row.astype(jnp.float32)
    seg_col = jnp.transpose(jnp.broadcast_to(seg_row, (LANES, chans)))
    same = across(seg_col, chans) == seg_row
    earlier = same & (iota((chans, chans), 1) < iota((chans, chans), 0))
    taken = jnp.dot(jnp.where(earlier, 1.0, 0.0).astype(jnp.bfloat16),
                    jnp.ones((chans, LANES), jnp.bfloat16), preferred_element_type=jnp.float32)
    lead = across(jnp.where((taken == 0.0) & (seg_col >= 0.0), 1.0, 0.0), chans)
    return seg_col, jnp.where(same, lead, 0.0).astype(jnp.bfloat16)


def scales(seg_col, pre_ref):
    energies, levels = pre_ref.shape
    picks = across(seg_col, levels) == iota((seg_col.shape[0], levels), 1).astype(jnp.float32)
    picks = jnp.where(picks, 1.0, 0.0).astype(jnp.bfloat16)
    own = lax.dot_general(picks, jnp.concatenate(split3(pre_ref[...]), axis=0), (((1,), (1,)), ((), ())),
                          preferred_element_type=jnp.float32)
    return jnp.dot(own.astype(jnp.bfloat16), spread_lanes(energies), preferred_element_type=jnp.float32)


def rowsums(block, blocks, energies, real_ref, imag_ref, same_ref, rows_ref):
    chans = same_ref.shape[0]
    jgrp = lax.axis_index("y") * lax.axis_size("x") + lax.axis_index("x")
    factor = (2 * (jgrp * blocks + block) + 1).astype(jnp.float32)
    delta = jnp.where(iota((LANES, LANES), 0) == iota((LANES, LANES), 1), 1.0, 0.0)
    for e in energies:
        real = real_ref[e].astype(jnp.float32)
        imag = imag_ref[e].astype(jnp.float32)
        on = [delta - real[k:k + LANES, k:k + LANES] for k in range(0, chans, LANES)]
        real = jnp.concatenate([
            jnp.concatenate([on[0], real[:LANES, LANES:]], axis=1),
            jnp.concatenate([real[LANES:, :LANES], on[1]], axis=1)], axis=0)
        weighted = ((real ** 2 + imag ** 2) * factor).astype(jnp.bfloat16)
        rowsum = jnp.dot(same_ref[...], weighted, preferred_element_type=jnp.float32)
        rows_ref[e] = rowsum.astype(jnp.bfloat16)


def share_kernel(count_hbm, level_hbm, real_hbm, imag_hbm, pre_hbm, max_hbm, *refs):
    blocks, chans = level_hbm.shape
    outs, refs = refs[:5 * blocks], refs[5 * blocks:]
    (real_ref, imag_ref, count_ref, level_ref, pre_ref, max_ref,
     rows_ref, same_ref, scale_ref, weight_ref, wide_ref, part_sem, small_sem) = refs
    temps, energies = max_ref.shape
    half = chans // 2
    width = energies * GROUP
    core = lax.axis_index("core")
    smalls = []
    for i, pair in enumerate(((count_hbm, count_ref), (level_hbm, level_ref),
                              (pre_hbm, pre_ref), (max_hbm, max_ref))):
        smalls.append(pltpu.make_async_copy(*pair, small_sem.at[i]))
        smalls[-1].start()
    parts = [[] for _ in range(blocks)]
    for block in range(blocks):
        for step, (low, high) in enumerate(PLAN[block]):
            at = pl.ds(low, high - low)
            parts[block].append([
                pltpu.make_async_copy(x_hbm.at[block, at], x_ref.at[block, at], part_sem.at[i, block, step])
                for i, (x_hbm, x_ref) in enumerate(((real_hbm, real_ref), (imag_hbm, imag_ref)))
            ])
            for copy in parts[block][step]:
                copy.start()
    for copy in smalls[:2]:
        copy.wait()
    seg_cols = []
    for block in range(blocks):
        seg_col, same_ref[block] = leaders(block, count_ref, level_ref)
        seg_cols.append(seg_col)
    for block in range(blocks):
        for (low, high), copies in zip(PLAN[block], parts[block]):
            for copy in copies:
                copy.wait()
            rowsums(block, blocks, range(low, high), real_ref.at[block], imag_ref.at[block],
                    same_ref.at[block], rows_ref.at[block])
        if block == 0:
            for copy in smalls[2:]:
                copy.wait()
            wide_ref[...] = jnp.dot(jnp.concatenate(split3(max_ref[...]), axis=1), spread_lanes(energies),
                                    preferred_element_type=jnp.float32)
            hit = iota((GROUP, width), 1) % GROUP == iota((GROUP, width), 0)
            for s, t in enumerate(order(lax.axis_index("z"), core)):
                t = lax.rem(t + temps, temps)
                weight_ref[s * GROUP:(s + 1) * GROUP, :] = jnp.where(hit, wide_ref[pl.ds(t, 1), :], 0.0)
        scale_ref[block] = scales(seg_cols[block], pre_ref)
        send_ref, keep_ref, send_near, keep_near, own_ref = outs[block::blocks]
        for front, back, at in groups(chans, core):
            total = mix(rows_ref.at[block], scale_ref.at[block], weight_ref[...], at)
            low, mine = front % half, front < half
            for k in range(2):
                keep_near[k * chans + front:k * chans + front + GROUP, :] = total[k]
                send_near[k * chans + back:k * chans + back + GROUP, :] = total[2 + k]
                own_ref[k * chans + front:k * chans + front + GROUP, :] = total[4 + k]
                first_ref = keep_ref if mine else send_ref
                first_ref[k * half + low:k * half + low + GROUP, :] = total[6 + k if mine else 7 - k]


def choose_kernel(count_ref, level_ref, picks_ref, columns_ref):
    blocks, chans = level_ref.shape
    half = chans // 2
    core = lax.axis_index("core")
    levels = columns_ref.shape[1]
    row = iota((levels // 2, chans), 0)
    wanted = row // 2 * 4 + core * 2 + row % 2
    for block in range(blocks):
        seg = jnp.where(iota((1, chans), 1) < count_ref[block], level_ref[pl.ds(block, 1), :], -1)
        columns_ref[block] = jnp.where(iota((levels, chans), 0) == seg, 1.0, 0.0).astype(jnp.bfloat16)
        turned = jnp.concatenate([seg[:, half:], seg[:, :half]], axis=1)
        seg = jnp.where(core == 0, seg, turned)
        picks_ref[block] = jnp.where(wanted == seg, 1.0, 0.0).astype(jnp.bfloat16)


def float_of(*shape):
    return jax.ShapeDtypeStruct(shape, jnp.float32)


def half_of(*shape):
    return jax.ShapeDtypeStruct(shape, jnp.bfloat16)


def share(counts, level_map, s_real, s_imag, prefactor, maxwell):
    blocks, energies, chans = s_real.shape[:3]
    temps = maxwell.shape[0]
    width = energies * GROUP
    args = (counts, level_map, s_real, s_imag, prefactor, maxwell)
    out = pl.pallas_call(
        share_kernel,
        out_shape=[float_of(chans, chans)] * (2 * blocks) + [float_of(2 * chans, chans)] * (3 * blocks),
        in_specs=[pl.BlockSpec(memory_space=pltpu.HBM)] * 6,
        out_specs=[pl.BlockSpec(memory_space=pltpu.VMEM)] * (5 * blocks),
        scratch_shapes=[
            pltpu.VMEM(s_real.shape, jnp.bfloat16),
            pltpu.VMEM(s_imag.shape, jnp.bfloat16),
            pltpu.SMEM(counts.shape, jnp.int32),
            pltpu.VMEM(level_map.shape, jnp.int32),
            pltpu.VMEM(prefactor.shape, jnp.float32),
            pltpu.VMEM(maxwell.shape, jnp.float32),
            pltpu.VMEM(s_real.shape, jnp.bfloat16),
            pltpu.VMEM((blocks, chans, chans), jnp.bfloat16),
            pltpu.VMEM((blocks, chans, width), jnp.float32),
            pltpu.VMEM((temps * GROUP, width), jnp.float32),
            pltpu.VMEM((temps, width), jnp.float32),
            pltpu.SemaphoreType.DMA((2, blocks, 2)),
            pltpu.SemaphoreType.DMA((4,)),
        ],
        compiler_params=pltpu.CompilerParams(vmem_limit_bytes=24 * 2**20),
        name="share",
    )(*[pltpu.with_memory_space_constraint(x, pltpu.HBM) for x in args])
    return [out[i * blocks:(i + 1) * blocks] for i in range(5)]


def choose(counts, level_map, levels):
    blocks, chans = level_map.shape
    return pl.pallas_call(
        choose_kernel,
        out_shape=[half_of(blocks, levels // 2, chans), half_of(blocks, levels, chans)],
        in_specs=[pl.BlockSpec(memory_space=pltpu.SMEM), pl.BlockSpec(memory_space=pltpu.VMEM)],
        out_specs=[pl.BlockSpec(memory_space=pltpu.VMEM)] * 2,
        compiler_params=pltpu.CompilerParams(vmem_limit_bytes=16 * 2**20),
        name="choose",
    )(counts, level_map)


def spread_kernel(block, picks_ref, columns_ref, mine_ref, other_ref, *refs):
    out_ref = refs[-1]
    size, share = out_ref.shape[0], out_ref.shape[1] // 2
    chans = columns_ref.shape[2]
    half = chans // 2
    for k in range(2):
        low = k * chans
        both = mine_ref[low:low + chans] + jnp.concatenate(
            [other_ref[low + half:low + chans], other_ref[low:low + half]], axis=0)
        hi, lo = split2(both)
        wide = lax.dot_general(jnp.concatenate([hi, lo], axis=0), columns_ref[block], (((1,), (1,)), ((), ())),
                               preferred_element_type=jnp.float32)
        hi, lo = split2(wide[:chans] + wide[chans:])
        term = jnp.dot(picks_ref[block], hi, preferred_element_type=jnp.float32)
        term += jnp.dot(picks_ref[block], lo, preferred_element_type=jnp.float32)
        term = term.reshape(size, share, -1)
        at = slice(k * share, (k + 1) * share)
        out_ref[:, at, :] = term if len(refs) == 1 else refs[0][:, at, :] + term


def spread(block, size, picks, columns, *parts):
    whole = pl.BlockSpec(memory_space=pltpu.VMEM)
    rows, levels = picks.shape[1], columns.shape[1]
    return pl.pallas_call(
        functools.partial(spread_kernel, block),
        out_shape=float_of(size, 2 * rows // size, levels),
        in_specs=[whole] * (2 + len(parts)),
        out_specs=whole,
        compiler_params=pltpu.CompilerParams(vmem_limit_bytes=16 * 2**20),
        name="spread",
    )(picks, columns, *parts)


def body(s_real, s_imag, level_map, channel_count, prefactor, maxwell):
    chans, levels = s_real.shape[2], prefactor.shape[0]
    half = chans // 2
    n = lax.axis_size("z")
    size = lax.axis_size("y") * lax.axis_size("x")
    swap = [(0, 1), (1, 0)]
    ring = [(2 * i, (i + 1) % n * 2) for i in range(n)]
    ring += [(2 * i + 1, (i - 1) % n * 2 + 1) for i in range(n)]

    def move(x):
        return lax.ppermute(x, ("z", "core"), ring)

    send, keep, send_near, keep_near, own = share(
        channel_count, level_map, s_real, s_imag, prefactor.T, maxwell)
    others = [lax.ppermute(x, "core", swap) for x in send]
    send_near, others = lax.optimization_barrier((send_near, others))
    mine = []
    for block in range(len(send)):
        carry = move(keep[block] + others[block])
        near = keep_near[block] + lax.ppermute(send_near[block], "core", swap)
        carry = move(jnp.concatenate([near[:half] + carry[:half], near[half:chans],
                                      near[chans:chans + half] + carry[half:], near[chans + half:]]))
        mine.append(carry + own[block])
    others = [lax.ppermute(x, "core", swap) for x in mine]
    picks, columns = choose(channel_count, level_map, levels)
    part = spread(0, size, picks, columns, mine[0], others[0])
    part = spread(1, size, picks, columns, mine[1], others[1], part)
    part = lax.all_to_all(part, ("y", "x"), 0, 0, tiled=True).sum(0)
    part = part.reshape(2, n, -1, levels).transpose(1, 0, 2, 3)
    part = lax.all_to_all(part, "z", 0, 0, tiled=True)
    part = part[:, 0] + jnp.roll(part[:, 1], 4, axis=0)
    return jnp.transpose(part, (1, 0, 2))


def solution(mesh):
    fine = Mesh(mesh.devices.reshape(4, 4, 8, 2), ("y", "x", "z", "core"))
    jgrp, energy = ("y", "x"), ("z", "core")
    in_specs = (
        P(jgrp, energy, None, None),
        P(jgrp, energy, None, None),
        P(jgrp, None),
        P(jgrp),
        P(None, energy),
        P(None, energy),
    )
    out_specs = P(("y", "x", "z", "core"), None, None)
    return jax.shard_map(body, mesh=fine, in_specs=in_specs, out_specs=out_specs, check_vma=False)
```

time: 80.1 us -> 77.2 us (0.964)
  waiting for transfers between devices: 30.3 us -> 21.1 us
  blocking collectives: 30.8 us -> 37.7 us
    ppermute x8 -> x4, waiting for transfers between devices: 28.5 us -> 19.6 us  [move(): return lax.ppermute(x, ('z', 'core'), ring)]
    all_to_all x1, blocking collectives: 17.7 us -> 23.6 us  [body(): part = lax.all_to_all(part, ('y', 'x'), 0, 0, tiled=True).sum(0)]
    ppermute x2, waiting for transfers between devices: 1.51 us -> 0.12 us  [body(): others = [lax.ppermute(x, 'core', swap) for x in mine]]
    ppermute x5 -> x4, waiting for transfers between devices: 0.27 us -> 1.4 us  [the longest x2 1.4 us: body(): others = [lax.ppermute(x, 'core', swap) for x in send]]
    all_to_all x1, blocking collectives: 13 us -> 14 us  [body(): part = lax.all_to_all(part, 'z', 0, 0, tiled=True)]
    ppermute x8 -> x4, starting transfers between devices: 2.76 us -> 2.24 us  [move(): return lax.ppermute(x, ('z', 'core'), ring)]
    pallas_call x3 -> x4, Pallas kernels: 9.92 us -> 9.6 us  [the longest x1 6.85 us: share(): pl.pallas_call(share_kernel, out_shape=[float_of(chans, chans)] * (2 * bl...]
    ppermute x5 -> x4, starting transfers between devices: 4.69 us -> 4.75 us  [the longest x2 4.16 us: body(): near = keep_near[block] + lax.ppermute(send_near[block], 'core', swap)]
  transfers between devices with their start and end apart: 15 -> 10, of which waited for: 10 -> 7; matrix products, arithmetic and copies ran while one was open for 1% -> 1% of each run, Pallas kernels for 2% -> 2%
where the time goes in v1:
time: 77.2 us; the launch traced here: 77.1 us
  blocking collectives  37.7 us (49%)
  waiting for transfers between devices  21.1 us (27%)
  Pallas kernels  9.6 us (12%)
  starting transfers between devices  7.18 us (9%)
    all_to_all x1, blocking collectives, body(): part = lax.all_to_all(part, ('y', 'x'), 0, 0, tiled=True).sum(0)  23.6 us
    ppermute x4, waiting for transfers between devices, move(): return lax.ppermute(x, ('z', 'core'), ring)  19.6 us
    all_to_all x1, blocking collectives, body(): part = lax.all_to_all(part, 'z', 0, 0, tiled=True)  14 us
    pallas_call x1, Pallas kernels, share(): pl.pallas_call(share_kernel, out_shape=[float_of(chans, chans)] * (2 * bl...  6.85 us
    ppermute x2, starting transfers between devices, body(): near = keep_near[block] + lax.ppermute(send_near[block], 'core', swap)  4.16 us
    ppermute x4, starting transfers between devices, move(): return lax.ppermute(x, ('z', 'core'), ring)  2.24 us
    pallas_call x2, Pallas kernels, spread(): pl.pallas_call(functools.partial(spread_kernel, block), out_shape=float_o...  2.03 us
  transfers between devices with their start and end apart: 10, of which 7 were waited for; matrix products, arithmetic and copies ran while one was open for 1% of the time, Pallas kernels for 2%

profile of v1, /device:TPU:2, one launch (start us, length us, event | category | flops | bytes accessed | tf_op | source)
XLA Modules:
  0.0 77.1 jit_solution(2362324390039639678)
XLA Ops:
  0.0 6.8 %share.1 = (f32[256,256]{1,0:T(8,128)S(1)}, f32[256,256]{1,0:T(8,128)S(1)}, f32[256,256]{1,0:T(8,128)S(1)}, f32[256,256]{1,0:T(8,128)S(1)}, f32[512,256]{1,0:T(8...) custom-call(s32[2]{0:T(128)} %count_hbm.1, ...), custom_call_target="tpu_custom_call" | custom-call | tf_op jit(solution)/shard_map/share/pallas_call | solution.py:189
  6.9 0.1 collective-permute-start
  7.0 0.5 collective-permute-start.1
  7.5 1.0 %collective-permute-done = f32[256,256]{1,0:T(8,128)S(1)} collective-permute-done((f32[256,256]{1,0:T(8,128)S(1)}, f32[256,256]{1,0:T(8,128)S(1)}, u32[]{:S(2)}, u32[]{:S(2)}) %collective-permute-start) | collective-permute-done | bytes 262176 | tf_op jit(solution)/shard_map/ppermute | solution.py:274
  8.5 0.4 collective-permute-done.1
  8.9 0.1 collective-permute-start.6
  9.0 2.0 %collective-permute-start.7 = (f32[256,256]{1,0:T(8,128)S(1)}, f32[256,256]{1,0:T(8,128)S(1)}, u32[]{:S(2)}, u32[]{:S(2)}) collective-permute-start(f32[256,256]{1,0:T(8,128)S(1)} %add.39), channel_id=1, source_target_pairs={{0,2},{2,4},{4,6},{6,8},{8,10},{10,12},{12,14},{14,0},{1,15},{3,1}... | collective-permute-start | bytes 786440 | tf_op jit(solution)/shard_map/ppermute | solution.py:270
  11.0 4.0 %collective-permute-start.2 = (f32[512,256]{1,0:T(8,128)S(1)}, f32[512,256]{1,0:T(8,128)S(1)}, u32[]{:S(2)}, u32[]{:S(2)}) collective-permute-start(f32[512,256]{1,0:T(8,128)S(1)} %get-tuple-element.28), channel_id=1, source_target_pairs={{0,1},{1,0},{2,3},{3,2},{4,5},{5,4},{6,7},{7,6},{8,9},{9,8},{10,11... | collective-permute-start | bytes 1572872 | tf_op jit(solution)/shard_map/ppermute | solution.py:279
  15.1 0.1 collective-permute-start.3
  15.2 0.1 add.38
  15.3 4.0 %collective-permute-done.7 = f32[256,256]{1,0:T(8,128)S(1)} collective-permute-done((f32[256,256]{1,0:T(8,128)S(1)}, f32[256,256]{1,0:T(8,128)S(1)}, u32[]{:S(2)}, u32[]{:S(2)}) %collective-permute-start.7) | collective-permute-done | bytes 262176 | tf_op jit(solution)/shard_map/ppermute | solution.py:270
  19.3 0.1 slice_add_fusion.1
  19.4 0.0 copy-start
  19.4 0.1 collective-permute-start.8
  19.5 0.1 add.33
  19.6 3.1 %collective-permute-done.3 = f32[256,256]{1,0:T(8,128)S(1)} collective-permute-done((f32[256,256]{1,0:T(8,128)S(1)}, f32[256,256]{1,0:T(8,128)S(1)}, u32[]{:S(2)}, u32[]{:S(2)}) %collective-permute-start.3) | collective-permute-done | bytes 262176 | tf_op jit(solution)/shard_map/ppermute | solution.py:270
  22.7 0.1 slice_add_fusion.3
  22.8 0.1 collective-permute-start.4
  22.9 7.0 %collective-permute-done.8 = f32[512,256]{1,0:T(8,128)S(1)} collective-permute-done((f32[512,256]{1,0:T(8,128)S(1)}, f32[512,256]{1,0:T(8,128)S(1)}, u32[]{:S(2)}, u32[]{:S(2)}) %collective-permute-start.8) | collective-permute-done | bytes 524320 | tf_op jit(solution)/shard_map/ppermute | solution.py:270
  29.9 0.1 add.42.mine_ref
  30.0 0.1 collective-permute-start.9
  30.1 5.4 %collective-permute-done.4 = f32[512,256]{1,0:T(8,128)S(1)} collective-permute-done((f32[512,256]{1,0:T(8,128)S(1)}, f32[512,256]{1,0:T(8,128)S(1)}, u32[]{:S(2)}, u32[]{:S(2)}) %collective-permute-start.4) | collective-permute-done | bytes 524320 | tf_op jit(solution)/shard_map/ppermute | solution.py:270
  35.5 0.1 add.37.mine_ref
  35.6 0.1 collective-permute-start.5
  35.7 0.7 choose.1
  36.4 1.0 %spread.2.refs_0_ = f32[16,32,512]{2,1,0:T(8,128)S(1)} custom-call(bf16[2,256,256]{2,1,0:T(8,128)(2,1)S(1)} %get-tuple-element.21.picks_ref, bf16[2,512,256]{2,1,0:T(8,128)(2,1)S(1)} %get-tuple-element.22.columns_ref, f32[512,256]{1,0:T(8,128)S(1)} %add.42.mine_ref, f32[512,256]{1,0:T(8,128)S(1)} %collective-permute-done.9.other_ref), custom_call_target="tpu_custom_call" | custom-call | tf_op jit(solution)/shard_map/spread/pallas_call | solution.py:250
  37.5 0.1 collective-permute-done.5.other_ref
  37.6 1.0 %spread.3 = f32[16,32,512]{2,1,0:T(8,128)S(1)} custom-call(bf16[2,256,256]{2,1,0:T(8,128)(2,1)S(1)} %get-tuple-element.21.picks_ref, bf16[2,512,256]{2,1,0:T(8,128)(2,1)S(1)} %get-tuple-element.22.columns_ref, f32[512,256]{1,0:T(8,128)S(1)} %add.37.mine_ref, f32[512,256]{1,0:T(8,128)S(1)} %collective-permute-done.5.other_ref, f32[16,32,512]{2,1,0:T(8,128)S(1)} %spread.2.refs_0_), custom_call_target="tpu_custom_call" | custom-call | tf_op jit(solution)/shard_map/spread/pallas_call | solution.py:250
  38.6 23.6 %all_to_all.10 = f32[16,32,512]{2,1,0:T(8,128)S(1)} all-to-all(f32[16,32,512]{2,1,0:T(8,128)S(1)} %spread.3), channel_id=1, replica_groups=mesh['y'=4,'x'=4,'z'=8,'core'=2] {'y','x'}, dimensions={0} | all-to-all | bytes 2097152 | tf_op jit(solution)/shard_map/all_to_all | solution.py:287
  62.2 0.1 reduce_sum.9
  62.4 14.0 %all_to_all.11 = f32[8,2,2,512]{3,2,1,0:T(2,128)S(1)} all-to-all(f32[8,2,2,512]{3,2,1,0:T(2,128)S(1)} %copy.8), channel_id=1, replica_groups=mesh['y'=4,'x'=4,'z'=8,'core'=2] {'z'}, dimensions={0} | all-to-all | bytes 131072 | tf_op jit(solution)/shard_map/all_to_all | solution.py:289
  76.4 0.6 copy.11
  (14 shorter events, 0.2 us)
Async XLA Ops:
  6.9 1.6 %collective-permute-start = (f32[256,256]{1,0:T(8,128)S(1)}, f32[256,256]{1,0:T(8,128)S(1)}, u32[]{:S(2)}, u32[]{:S(2)}) collective-permute-start(f32[256,256]{1,0:T(8,128)S(1)} %get-tuple-element.26), channel_id=1, source_target_pairs={{0,1},{1,0},{2,3},{3,2},{4,5},{5,4},{6,7},{7,6},{8,9},{9,8},{10,11... | collective-permute-start | bytes 786440 | tf_op jit(solution)/shard_map/ppermute | solution.py:274
  7.0 1.9 %collective-permute-start.1 = (f32[256,256]{1,0:T(8,128)S(1)}, f32[256,256]{1,0:T(8,128)S(1)}, u32[]{:S(2)}, u32[]{:S(2)}) collective-permute-start(f32[256,256]{1,0:T(8,128)S(1)} %get-tuple-element.27), channel_id=1, source_target_pairs={{0,1},{1,0},{2,3},{3,2},{4,5},{5,4},{6,7},{7,6},{8,9},{9,8},{10,11... | collective-permute-start | bytes 786440 | tf_op jit(solution)/shard_map/ppermute | solution.py:274
  8.9 6.3 %collective-permute-start.6 = (f32[512,256]{1,0:T(8,128)S(1)}, f32[512,256]{1,0:T(8,128)S(1)}, u32[]{:S(2)}, u32[]{:S(2)}) collective-permute-start(f32[512,256]{1,0:T(8,128)S(1)} %get-tuple-element.33), channel_id=1, source_target_pairs={{0,1},{1,0},{2,3},{3,2},{4,5},{5,4},{6,7},{7,6},{8,9},{9,8},{10,11... | collective-permute-start | bytes 1572872 | tf_op jit(solution)/shard_map/ppermute | solution.py:279
  9.0 10.3 %collective-permute-start.7 = (f32[256,256]{1,0:T(8,128)S(1)}, f32[256,256]{1,0:T(8,128)S(1)}, u32[]{:S(2)}, u32[]{:S(2)}) collective-permute-start(f32[256,256]{1,0:T(8,128)S(1)} %add.39), channel_id=1, source_target_pairs={{0,2},{2,4},{4,6},{6,8},{8,10},{10,12},{12,14},{14,0},{1,15},{3,1}... | collective-permute-start | bytes 786440 | tf_op jit(solution)/shard_map/ppermute | solution.py:270
  11.0 8.5 %collective-permute-start.2 = (f32[512,256]{1,0:T(8,128)S(1)}, f32[512,256]{1,0:T(8,128)S(1)}, u32[]{:S(2)}, u32[]{:S(2)}) collective-permute-start(f32[512,256]{1,0:T(8,128)S(1)} %get-tuple-element.28), channel_id=1, source_target_pairs={{0,1},{1,0},{2,3},{3,2},{4,5},{5,4},{6,7},{7,6},{8,9},{9,8},{10,11... | collective-permute-start | bytes 1572872 | tf_op jit(solution)/shard_map/ppermute | solution.py:279
  15.1 7.7 %collective-permute-start.3 = (f32[256,256]{1,0:T(8,128)S(1)}, f32[256,256]{1,0:T(8,128)S(1)}, u32[]{:S(2)}, u32[]{:S(2)}) collective-permute-start(f32[256,256]{1,0:T(8,128)S(1)} %add.34), channel_id=1, source_target_pairs={{0,2},{2,4},{4,6},{6,8},{8,10},{10,12},{12,14},{14,0},{1,15},{3,1}... | collective-permute-start | bytes 786440 | tf_op jit(solution)/shard_map/ppermute | solution.py:270
  19.4 16.3 %copy-start = (s32[2,256]{1,0:T(2,128)S(1)}, s32[2,256]{1,0:T(2,128)}, u32[]{:S(2)}) copy-start(s32[2,256]{1,0:T(2,128)} %level_hbm.1) | copy-start | bytes 6148
  19.4 16.3 %copy-start.1 = (s32[2]{0:T(128)S(1)}, s32[2]{0:T(128)}, u32[]{:S(2)}) copy-start(s32[2]{0:T(128)} %count_hbm.1) | copy-start | bytes 28
  19.4 10.5 %collective-permute-start.8 = (f32[512,256]{1,0:T(8,128)S(1)}, f32[512,256]{1,0:T(8,128)S(1)}, u32[]{:S(2)}, u32[]{:S(2)}) collective-permute-start(f32[512,256]{1,0:T(8,128)S(1)} %pad_maximum_fusion.1), channel_id=1, source_target_pairs={{0,2},{2,4},{4,6},{6,8},{8,10},{10,12},{12,14},{14,0},{1,15},{3,1}... | collective-permute-start | bytes 1572872 | tf_op jit(solution)/shard_map/ppermute | solution.py:270
  22.8 12.7 %collective-permute-start.4 = (f32[512,256]{1,0:T(8,128)S(1)}, f32[512,256]{1,0:T(8,128)S(1)}, u32[]{:S(2)}, u32[]{:S(2)}) collective-permute-start(f32[512,256]{1,0:T(8,128)S(1)} %pad_maximum_fusion), channel_id=1, source_target_pairs={{0,2},{2,4},{4,6},{6,8},{8,10},{10,12},{12,14},{14,0},{1,15},{3,1}... | collective-permute-start | bytes 1572872 | tf_op jit(solution)/shard_map/ppermute | solution.py:270
  30.0 6.5 %collective-permute-start.9 = (f32[512,256]{1,0:T(8,128)S(1)}, f32[512,256]{1,0:T(8,128)S(1)}, u32[]{:S(2)}, u32[]{:S(2)}) collective-permute-start(f32[512,256]{1,0:T(8,128)S(1)} %add.42.mine_ref), channel_id=1, source_target_pairs={{0,1},{1,0},{2,3},{3,2},{4,5},{5,4},{6,7},{7,6},{8,9},{9,8},{10,11... | collective-permute-start | bytes 1572872 | tf_op jit(solution)/shard_map/ppermute | solution.py:283
  35.6 2.0 %collective-permute-start.5 = (f32[512,256]{1,0:T(8,128)S(1)}, f32[512,256]{1,0:T(8,128)S(1)}, u32[]{:S(2)}, u32[]{:S(2)}) collective-permute-start(f32[512,256]{1,0:T(8,128)S(1)} %add.37.mine_ref), channel_id=1, source_target_pairs={{0,1},{1,0},{2,3},{3,2},{4,5},{5,4},{6,7},{7,6},{8,9},{9,8},{10,11... | collective-permute-start | bytes 1572872 | tf_op jit(solution)/shard_map/ppermute | solution.py:283

commit v2 on v1

--- a/solution.py
+++ b/solution.py
@@ -145,6 +145,7 @@
             for s, t in enumerate(order(lax.axis_index("z"), core)):
                 t = lax.rem(t + temps, temps)
                 weight_ref[s * GROUP:(s + 1) * GROUP, :] = jnp.where(hit, wide_ref[pl.ds(t, 1), :], 0.0)
+    for block in range(blocks):
         scale_ref[block] = scales(seg_cols[block], pre_ref)
         send_ref, keep_ref, send_near, keep_near, own_ref = outs[block::blocks]
         for front, back, at in groups(chans, core):
@@ -272,7 +273,7 @@
     send, keep, send_near, keep_near, own = share(
         channel_count, level_map, s_real, s_imag, prefactor.T, maxwell)
     others = [lax.ppermute(x, "core", swap) for x in send]
-    send_near, others = lax.optimization_barrier((send_near, others))
+    send_near, others[0] = lax.optimization_barrier((send_near, others[0]))
     mine = []
     for block in range(len(send)):
         carry = move(keep[block] + others[block])

time: 77.2 us -> 77.3 us (level)
  transfers between devices with their start and end apart: 10 -> 10, of which waited for: 7 -> 6; matrix products, arithmetic and copies ran while one was open for 1% -> 1% of each run, Pallas kernels for 2% -> 2%
where the time goes in v2:
time: 77.3 us; the launch traced here: 77.2 us
  blocking collectives  37.7 us (49%)
  waiting for transfers between devices  21.5 us (28%)
  Pallas kernels  9.7 us (13%)
  starting transfers between devices  6.83 us (9%)
    all_to_all x1, blocking collectives, body(): part = lax.all_to_all(part, ('y', 'x'), 0, 0, tiled=True).sum(0)  23.6 us
    ppermute x4, waiting for transfers between devices, move(): return lax.ppermute(x, ('z', 'core'), ring)  19.8 us
    all_to_all x1, blocking collectives, body(): part = lax.all_to_all(part, 'z', 0, 0, tiled=True)  14 us
    pallas_call x1, Pallas kernels, share(): pl.pallas_call(share_kernel, out_shape=[float_of(chans, chans)] * (2 * bl...  6.95 us
    ppermute x2, starting transfers between devices, body(): near = keep_near[block] + lax.ppermute(send_near[block], 'core', swap)  3.93 us
    ppermute x4, starting transfers between devices, move(): return lax.ppermute(x, ('z', 'core'), ring)  2.24 us
    pallas_call x2, Pallas kernels, spread(): pl.pallas_call(functools.partial(spread_kernel, block), out_shape=float_o...  2.03 us
  transfers between devices with their start and end apart: 10, of which 6 were waited for; matrix products, arithmetic and copies ran while one was open for 1% of the time, Pallas kernels for 2%

profile of v2, /device:TPU:2, one launch (start us, length us, event | category | flops | bytes accessed | tf_op | source)
XLA Modules:
  0.0 77.2 jit_solution(12399145929671353036)
XLA Ops:
  0.0 6.9 %share.1 = (f32[256,256]{1,0:T(8,128)S(1)}, f32[256,256]{1,0:T(8,128)S(1)}, f32[256,256]{1,0:T(8,128)S(1)}, f32[256,256]{1,0:T(8,128)S(1)}, f32[512,256]{1,0:T(8...) custom-call(s32[2]{0:T(128)} %count_hbm.1, ...), custom_call_target="tpu_custom_call" | custom-call | tf_op jit(solution)/shard_map/share/pallas_call | solution.py:190
  7.0 0.1 collective-permute-start
  7.1 1.5 %collective-permute-done = f32[256,256]{1,0:T(8,128)S(1)} collective-permute-done((f32[256,256]{1,0:T(8,128)S(1)}, f32[256,256]{1,0:T(8,128)S(1)}, u32[]{:S(2)}, u32[]{:S(2)}) %collective-permute-start) | collective-permute-done | bytes 262176 | tf_op jit(solution)/shard_map/ppermute | solution.py:275
  8.6 0.1 collective-permute-start.6
  8.7 0.4 collective-permute-start.2
  9.1 2.0 %collective-permute-start.7 = (f32[256,256]{1,0:T(8,128)S(1)}, f32[256,256]{1,0:T(8,128)S(1)}, u32[]{:S(2)}, u32[]{:S(2)}) collective-permute-start(f32[256,256]{1,0:T(8,128)S(1)} %add.39), channel_id=1, source_target_pairs={{0,2},{2,4},{4,6},{6,8},{8,10},{10,12},{12,14},{14,0},{1,15},{3,1}... | collective-permute-start | bytes 786440 | tf_op jit(solution)/shard_map/ppermute | solution.py:271
  11.1 3.8 %collective-permute-start.1 = (f32[512,256]{1,0:T(8,128)S(1)}, f32[512,256]{1,0:T(8,128)S(1)}, u32[]{:S(2)}, u32[]{:S(2)}) collective-permute-start(f32[512,256]{1,0:T(8,128)S(1)} %get-tuple-element.26), channel_id=1, source_target_pairs={{0,1},{1,0},{2,3},{3,2},{4,5},{5,4},{6,7},{7,6},{8,9},{9,8},{10,11... | collective-permute-start | bytes 1572872 | tf_op jit(solution)/shard_map/ppermute | solution.py:280
  15.0 0.1 collective-permute-start.3
  15.1 0.1 add.38
  15.1 4.3 %collective-permute-done.7 = f32[256,256]{1,0:T(8,128)S(1)} collective-permute-done((f32[256,256]{1,0:T(8,128)S(1)}, f32[256,256]{1,0:T(8,128)S(1)}, u32[]{:S(2)}, u32[]{:S(2)}) %collective-permute-start.7) | collective-permute-done | bytes 262176 | tf_op jit(solution)/shard_map/ppermute | solution.py:271
  19.4 0.1 slice_add_fusion.1
  19.5 0.0 copy-start
  19.5 0.0 copy-start.1
  19.5 0.1 collective-permute-start.8
  19.6 0.1 add.33
  19.7 2.9 %collective-permute-done.3 = f32[256,256]{1,0:T(8,128)S(1)} collective-permute-done((f32[256,256]{1,0:T(8,128)S(1)}, f32[256,256]{1,0:T(8,128)S(1)}, u32[]{:S(2)}, u32[]{:S(2)}) %collective-permute-start.3) | collective-permute-done | bytes 262176 | tf_op jit(solution)/shard_map/ppermute | solution.py:271
  22.6 0.1 slice_add_fusion.3
  22.7 0.1 collective-permute-start.4
  22.8 7.2 %collective-permute-done.8 = f32[512,256]{1,0:T(8,128)S(1)} collective-permute-done((f32[512,256]{1,0:T(8,128)S(1)}, f32[512,256]{1,0:T(8,128)S(1)}, u32[]{:S(2)}, u32[]{:S(2)}) %collective-permute-start.8) | collective-permute-done | bytes 524320 | tf_op jit(solution)/shard_map/ppermute | solution.py:271
  30.0 0.1 add.42.mine_ref
  30.1 0.1 collective-permute-start.9
  30.2 5.4 %collective-permute-done.4 = f32[512,256]{1,0:T(8,128)S(1)} collective-permute-done((f32[512,256]{1,0:T(8,128)S(1)}, f32[512,256]{1,0:T(8,128)S(1)}, u32[]{:S(2)}, u32[]{:S(2)}) %collective-permute-start.4) | collective-permute-done | bytes 524320 | tf_op jit(solution)/shard_map/ppermute | solution.py:271
  35.6 0.1 add.37.mine_ref
  35.7 0.1 collective-permute-start.5
  35.8 0.7 choose.1
  36.6 1.0 %spread.2.refs_0_ = f32[16,32,512]{2,1,0:T(8,128)S(1)} custom-call(bf16[2,256,256]{2,1,0:T(8,128)(2,1)S(1)} %get-tuple-element.20.picks_ref, bf16[2,512,256]{2,1,0:T(8,128)(2,1)S(1)} %get-tuple-element.21.columns_ref, f32[512,256]{1,0:T(8,128)S(1)} %add.42.mine_ref, f32[512,256]{1,0:T(8,128)S(1)} %collective-permute-done.9.other_ref), custom_call_target="tpu_custom_call" | custom-call | tf_op jit(solution)/shard_map/spread/pallas_call | solution.py:251
  37.6 0.1 collective-permute-done.5.other_ref
  37.7 1.0 %spread.3 = f32[16,32,512]{2,1,0:T(8,128)S(1)} custom-call(bf16[2,256,256]{2,1,0:T(8,128)(2,1)S(1)} %get-tuple-element.20.picks_ref, bf16[2,512,256]{2,1,0:T(8,128)(2,1)S(1)} %get-tuple-element.21.columns_ref, f32[512,256]{1,0:T(8,128)S(1)} %add.37.mine_ref, f32[512,256]{1,0:T(8,128)S(1)} %collective-permute-done.5.other_ref, f32[16,32,512]{2,1,0:T(8,128)S(1)} %spread.2.refs_0_), custom_call_target="tpu_custom_call" | custom-call | tf_op jit(solution)/shard_map/spread/pallas_call | solution.py:251
  38.7 23.6 %all_to_all.10 = f32[16,32,512]{2,1,0:T(8,128)S(1)} all-to-all(f32[16,32,512]{2,1,0:T(8,128)S(1)} %spread.3), channel_id=1, replica_groups=mesh['y'=4,'x'=4,'z'=8,'core'=2] {'y','x'}, dimensions={0} | all-to-all | bytes 2097152 | tf_op jit(solution)/shard_map/all_to_all | solution.py:288
  62.4 0.1 reduce_sum.9
  62.5 14.0 %all_to_all.11 = f32[8,2,2,512]{3,2,1,0:T(2,128)S(1)} all-to-all(f32[8,2,2,512]{3,2,1,0:T(2,128)S(1)} %copy.8), channel_id=1, replica_groups=mesh['y'=4,'x'=4,'z'=8,'core'=2] {'z'}, dimensions={0} | all-to-all | bytes 131072 | tf_op jit(solution)/shard_map/all_to_all | solution.py:290
  76.5 0.6 copy.11
  (14 shorter events, 0.2 us)
Async XLA Ops:
  7.0 1.6 %collective-permute-start = (f32[256,256]{1,0:T(8,128)S(1)}, f32[256,256]{1,0:T(8,128)S(1)}, u32[]{:S(2)}, u32[]{:S(2)}) collective-permute-start(f32[256,256]{1,0:T(8,128)S(1)} %get-tuple-element.25), channel_id=1, source_target_pairs={{0,1},{1,0},{2,3},{3,2},{4,5},{5,4},{6,7},{7,6},{8,9},{9,8},{10,11... | collective-permute-start | bytes 786440 | tf_op jit(solution)/shard_map/ppermute | solution.py:275
  8.6 6.5 %collective-permute-start.6 = (f32[512,256]{1,0:T(8,128)S(1)}, f32[512,256]{1,0:T(8,128)S(1)}, u32[]{:S(2)}, u32[]{:S(2)}) collective-permute-start(f32[512,256]{1,0:T(8,128)S(1)} %get-tuple-element.31), channel_id=1, source_target_pairs={{0,1},{1,0},{2,3},{3,2},{4,5},{5,4},{6,7},{7,6},{8,9},{9,8},{10,11... | collective-permute-start | bytes 1572872 | tf_op jit(solution)/shard_map/ppermute | solution.py:280
  8.7 6.2 %collective-permute-start.2 = (f32[256,256]{1,0:T(8,128)S(1)}, f32[256,256]{1,0:T(8,128)S(1)}, u32[]{:S(2)}, u32[]{:S(2)}) collective-permute-start(f32[256,256]{1,0:T(8,128)S(1)} %get-tuple-element.28), channel_id=1, source_target_pairs={{0,1},{1,0},{2,3},{3,2},{4,5},{5,4},{6,7},{7,6},{8,9},{9,8},{10,11... | collective-permute-start | bytes 786440 | tf_op jit(solution)/shard_map/ppermute | solution.py:275
  9.1 10.3 %collective-permute-start.7 = (f32[256,256]{1,0:T(8,128)S(1)}, f32[256,256]{1,0:T(8,128)S(1)}, u32[]{:S(2)}, u32[]{:S(2)}) collective-permute-start(f32[256,256]{1,0:T(8,128)S(1)} %add.39), channel_id=1, source_target_pairs={{0,2},{2,4},{4,6},{6,8},{8,10},{10,12},{12,14},{14,0},{1,15},{3,1}... | collective-permute-start | bytes 786440 | tf_op jit(solution)/shard_map/ppermute | solution.py:271
  11.1 8.5 %collective-permute-start.1 = (f32[512,256]{1,0:T(8,128)S(1)}, f32[512,256]{1,0:T(8,128)S(1)}, u32[]{:S(2)}, u32[]{:S(2)}) collective-permute-start(f32[512,256]{1,0:T(8,128)S(1)} %get-tuple-element.26), channel_id=1, source_target_pairs={{0,1},{1,0},{2,3},{3,2},{4,5},{5,4},{6,7},{7,6},{8,9},{9,8},{10,11... | collective-permute-start | bytes 1572872 | tf_op jit(solution)/shard_map/ppermute | solution.py:280
  15.0 7.7 %collective-permute-start.3 = (f32[256,256]{1,0:T(8,128)S(1)}, f32[256,256]{1,0:T(8,128)S(1)}, u32[]{:S(2)}, u32[]{:S(2)}) collective-permute-start(f32[256,256]{1,0:T(8,128)S(1)} %add.34), channel_id=1, source_target_pairs={{0,2},{2,4},{4,6},{6,8},{8,10},{10,12},{12,14},{14,0},{1,15},{3,1}... | collective-permute-start | bytes 786440 | tf_op jit(solution)/shard_map/ppermute | solution.py:271
  19.5 16.3 %copy-start = (s32[2,256]{1,0:T(2,128)S(1)}, s32[2,256]{1,0:T(2,128)}, u32[]{:S(2)}) copy-start(s32[2,256]{1,0:T(2,128)} %level_hbm.1) | copy-start | bytes 6148
  19.5 16.3 %copy-start.1 = (s32[2]{0:T(128)S(1)}, s32[2]{0:T(128)}, u32[]{:S(2)}) copy-start(s32[2]{0:T(128)} %count_hbm.1) | copy-start | bytes 28
  19.5 10.5 %collective-permute-start.8 = (f32[512,256]{1,0:T(8,128)S(1)}, f32[512,256]{1,0:T(8,128)S(1)}, u32[]{:S(2)}, u32[]{:S(2)}) collective-permute-start(f32[512,256]{1,0:T(8,128)S(1)} %pad_maximum_fusion.1), channel_id=1, source_target_pairs={{0,2},{2,4},{4,6},{6,8},{8,10},{10,12},{12,14},{14,0},{1,15},{3,1}... | collective-permute-start | bytes 1572872 | tf_op jit(solution)/shard_map/ppermute | solution.py:271
  22.7 12.9 %collective-permute-start.4 = (f32[512,256]{1,0:T(8,128)S(1)}, f32[512,256]{1,0:T(8,128)S(1)}, u32[]{:S(2)}, u32[]{:S(2)}) collective-permute-start(f32[512,256]{1,0:T(8,128)S(1)} %pad_maximum_fusion), channel_id=1, source_target_pairs={{0,2},{2,4},{4,6},{6,8},{8,10},{10,12},{12,14},{14,0},{1,15},{3,1}... | collective-permute-start | bytes 1572872 | tf_op jit(solution)/shard_map/ppermute | solution.py:271
  30.1 6.5 %collective-permute-start.9 = (f32[512,256]{1,0:T(8,128)S(1)}, f32[512,256]{1,0:T(8,128)S(1)}, u32[]{:S(2)}, u32[]{:S(2)}) collective-permute-start(f32[512,256]{1,0:T(8,128)S(1)} %add.42.mine_ref), channel_id=1, source_target_pairs={{0,1},{1,0},{2,3},{3,2},{4,5},{5,4},{6,7},{7,6},{8,9},{9,8},{10,11... | collective-permute-start | bytes 1572872 | tf_op jit(solution)/shard_map/ppermute | solution.py:284
  35.7 2.0 %collective-permute-start.5 = (f32[512,256]{1,0:T(8,128)S(1)}, f32[512,256]{1,0:T(8,128)S(1)}, u32[]{:S(2)}, u32[]{:S(2)}) collective-permute-start(f32[512,256]{1,0:T(8,128)S(1)} %add.37.mine_ref), channel_id=1, source_target_pairs={{0,1},{1,0},{2,3},{3,2},{4,5},{5,4},{6,7},{7,6},{8,9},{9,8},{10,11... | collective-permute-start | bytes 1572872 | tf_op jit(solution)/shard_map/ppermute | solution.py:284

commit v3 on v2

--- a/solution.py
+++ b/solution.py
@@ -274,15 +274,17 @@
         channel_count, level_map, s_real, s_imag, prefactor.T, maxwell)
     others = [lax.ppermute(x, "core", swap) for x in send]
     send_near, others[0] = lax.optimization_barrier((send_near, others[0]))
+    picks, columns = choose(channel_count, level_map, levels)
     mine = []
     for block in range(len(send)):
         carry = move(keep[block] + others[block])
         near = keep_near[block] + lax.ppermute(send_near[block], "core", swap)
         carry = move(jnp.concatenate([near[:half] + carry[:half], near[half:chans],
                                       near[chans:chans + half] + carry[half:], near[chans + half:]]))
+        if block == 0:
+            carry, picks, columns = lax.optimization_barrier((carry, picks, columns))
         mine.append(carry + own[block])
     others = [lax.ppermute(x, "core", swap) for x in mine]
-    picks, columns = choose(channel_count, level_map, levels)
     part = spread(0, size, picks, columns, mine[0], others[0])
     part = spread(1, size, picks, columns, mine[1], others[1], part)
     part = lax.all_to_all(part, ("y", "x"), 0, 0, tiled=True).sum(0)

time: 77.3 us -> 77 us (level)
  no operation moved by 1% of the time
where the time goes in v3:
time: 77 us; the launch traced here: 76.9 us
  blocking collectives  37.4 us (49%)
  waiting for transfers between devices  21.5 us (28%)
  Pallas kernels  9.7 us (13%)
  starting transfers between devices  6.83 us (9%)
    all_to_all x1, blocking collectives, body(): part = lax.all_to_all(part, ('y', 'x'), 0, 0, tiled=True).sum(0)  23.4 us
    ppermute x4, waiting for transfers between devices, move(): return lax.ppermute(x, ('z', 'core'), ring)  19.1 us
    all_to_all x1, blocking collectives, body(): part = lax.all_to_all(part, 'z', 0, 0, tiled=True)  14 us
    pallas_call x1, Pallas kernels, share(): pl.pallas_call(share_kernel, out_shape=[float_of(chans, chans)] * (2 * bl...  6.95 us
    ppermute x2, starting transfers between devices, body(): near = keep_near[block] + lax.ppermute(send_near[block], 'core', swap)  3.93 us
    ppermute x4, starting transfers between devices, move(): return lax.ppermute(x, ('z', 'core'), ring)  2.24 us
    pallas_call x2, Pallas kernels, spread(): pl.pallas_call(functools.partial(spread_kernel, block), out_shape=float_o...  2.03 us
  transfers between devices with their start and end apart: 10, of which 6 were waited for; matrix products, arithmetic and copies ran while one was open for 1% of the time, Pallas kernels for 2%

profile of v3, /device:TPU:2, one launch (start us, length us, event | category | flops | bytes accessed | tf_op | source)
XLA Modules:
  0.0 76.9 jit_solution(8014071067600873426)
XLA Ops:
  0.0 6.9 %share.1 = (f32[256,256]{1,0:T(8,128)S(1)}, f32[256,256]{1,0:T(8,128)S(1)}, f32[256,256]{1,0:T(8,128)S(1)}, f32[256,256]{1,0:T(8,128)S(1)}, f32[512,256]{1,0:T(8...) custom-call(s32[2]{0:T(128)} %count_ref.1, ...), custom_call_target="tpu_custom_call" | custom-call | tf_op jit(solution)/shard_map/share/pallas_call | solution.py:190
  7.0 0.1 collective-permute-start
  7.1 1.5 %collective-permute-done = f32[256,256]{1,0:T(8,128)S(1)} collective-permute-done((f32[256,256]{1,0:T(8,128)S(1)}, f32[256,256]{1,0:T(8,128)S(1)}, u32[]{:S(2)}, u32[]{:S(2)}) %collective-permute-start) | collective-permute-done | bytes 262176 | tf_op jit(solution)/shard_map/ppermute | solution.py:275
  8.6 0.1 collective-permute-start.1
  8.7 0.4 collective-permute-start.5
  9.1 2.0 %collective-permute-start.2 = (f32[256,256]{1,0:T(8,128)S(1)}, f32[256,256]{1,0:T(8,128)S(1)}, u32[]{:S(2)}, u32[]{:S(2)}) collective-permute-start(f32[256,256]{1,0:T(8,128)S(1)} %add.34), channel_id=1, source_target_pairs={{0,2},{2,4},{4,6},{6,8},{8,10},{10,12},{12,14},{14,0},{1,15},{3,1}... | collective-permute-start | bytes 786440 | tf_op jit(solution)/shard_map/ppermute | solution.py:271
  11.1 3.8 %collective-permute-start.4 = (f32[512,256]{1,0:T(8,128)S(1)}, f32[512,256]{1,0:T(8,128)S(1)}, u32[]{:S(2)}, u32[]{:S(2)}) collective-permute-start(f32[512,256]{1,0:T(8,128)S(1)} %get-tuple-element.35), channel_id=1, source_target_pairs={{0,1},{1,0},{2,3},{3,2},{4,5},{5,4},{6,7},{7,6},{8,9},{9,8},{10,11... | collective-permute-start | bytes 1572872 | tf_op jit(solution)/shard_map/ppermute | solution.py:281
  14.9 0.0 collective-permute-done.5
  15.0 0.1 collective-permute-start.6
  15.1 0.1 add.33
  15.1 4.3 %collective-permute-done.2 = f32[256,256]{1,0:T(8,128)S(1)} collective-permute-done((f32[256,256]{1,0:T(8,128)S(1)}, f32[256,256]{1,0:T(8,128)S(1)}, u32[]{:S(2)}, u32[]{:S(2)}) %collective-permute-start.2) | collective-permute-done | bytes 262176 | tf_op jit(solution)/shard_map/ppermute | solution.py:271
  19.4 0.1 slice_add_fusion.3
  19.5 0.1 collective-permute-start.3
  19.6 0.1 add.37
  19.7 2.9 %collective-permute-done.6 = f32[256,256]{1,0:T(8,128)S(1)} collective-permute-done((f32[256,256]{1,0:T(8,128)S(1)}, f32[256,256]{1,0:T(8,128)S(1)}, u32[]{:S(2)}, u32[]{:S(2)}) %collective-permute-start.6) | collective-permute-done | bytes 262176 | tf_op jit(solution)/shard_map/ppermute | solution.py:271
  22.6 0.1 slice_add_fusion.1
  22.7 0.1 collective-permute-start.7
  22.8 0.7 choose.1
  23.6 6.4 %collective-permute-done.3 = f32[512,256]{1,0:T(8,128)S(1)} collective-permute-done((f32[512,256]{1,0:T(8,128)S(1)}, f32[512,256]{1,0:T(8,128)S(1)}, u32[]{:S(2)}, u32[]{:S(2)}) %collective-permute-start.3) | collective-permute-done | bytes 524320 | tf_op jit(solution)/shard_map/ppermute | solution.py:271
  30.0 0.1 add.42.mine_ref
  30.1 0.1 collective-permute-start.9
  30.2 5.4 %collective-permute-done.7 = f32[512,256]{1,0:T(8,128)S(1)} collective-permute-done((f32[512,256]{1,0:T(8,128)S(1)}, f32[512,256]{1,0:T(8,128)S(1)}, u32[]{:S(2)}, u32[]{:S(2)}) %collective-permute-start.7) | collective-permute-done | bytes 524320 | tf_op jit(solution)/shard_map/ppermute | solution.py:271
  35.6 0.1 add.41.mine_ref
  35.7 0.1 collective-permute-start.8
  35.8 0.0 collective-permute-done.9.other_ref
  35.8 1.0 %spread.2.refs_0_ = f32[16,32,512]{2,1,0:T(8,128)S(1)} custom-call(bf16[2,256,256]{2,1,0:T(8,128)(2,1)S(1)} %get-tuple-element.32.picks_ref, bf16[2,512,256]{2,1,0:T(8,128)(2,1)S(1)} %get-tuple-element.33.columns_ref, f32[512,256]{1,0:T(8,128)S(1)} %add.42.mine_ref, f32[512,256]{1,0:T(8,128)S(1)} %collective-permute-done.9.other_ref), custom_call_target="tpu_custom_call" | custom-call | tf_op jit(solution)/shard_map/spread/pallas_call | solution.py:251
  36.8 0.9 %collective-permute-done.8.other_ref = f32[512,256]{1,0:T(8,128)S(1)} collective-permute-done((f32[512,256]{1,0:T(8,128)S(1)}, f32[512,256]{1,0:T(8,128)S(1)}, u32[]{:S(2)}, u32[]{:S(2)}) %collective-permute-start.8) | collective-permute-done | bytes 524320 | tf_op jit(solution)/shard_map/ppermute | solution.py:287
  37.7 1.0 %spread.3 = f32[16,32,512]{2,1,0:T(8,128)S(1)} custom-call(bf16[2,256,256]{2,1,0:T(8,128)(2,1)S(1)} %get-tuple-element.32.picks_ref, bf16[2,512,256]{2,1,0:T(8,128)(2,1)S(1)} %get-tuple-element.33.columns_ref, f32[512,256]{1,0:T(8,128)S(1)} %add.41.mine_ref, f32[512,256]{1,0:T(8,128)S(1)} %collective-permute-done.8.other_ref, f32[16,32,512]{2,1,0:T(8,128)S(1)} %spread.2.refs_0_), custom_call_target="tpu_custom_call" | custom-call | tf_op jit(solution)/shard_map/spread/pallas_call | solution.py:251
  38.7 23.4 %all_to_all.10 = f32[16,32,512]{2,1,0:T(8,128)S(1)} all-to-all(f32[16,32,512]{2,1,0:T(8,128)S(1)} %spread.3), channel_id=1, replica_groups=mesh['y'=4,'x'=4,'z'=8,'core'=2] {'y','x'}, dimensions={0} | all-to-all | bytes 2097152 | tf_op jit(solution)/shard_map/all_to_all | solution.py:290
  62.1 0.1 reduce_sum.9
  62.2 14.0 %all_to_all.11 = f32[8,2,2,512]{3,2,1,0:T(2,128)S(1)} all-to-all(f32[8,2,2,512]{3,2,1,0:T(2,128)S(1)} %copy.8), channel_id=1, replica_groups=mesh['y'=4,'x'=4,'z'=8,'core'=2] {'z'}, dimensions={0} | all-to-all | bytes 131072 | tf_op jit(solution)/shard_map/all_to_all | solution.py:292
  76.2 0.6 copy.11
  (14 shorter events, 0.2 us)
Async XLA Ops:
  7.0 1.6 %collective-permute-start = (f32[256,256]{1,0:T(8,128)S(1)}, f32[256,256]{1,0:T(8,128)S(1)}, u32[]{:S(2)}, u32[]{:S(2)}) collective-permute-start(f32[256,256]{1,0:T(8,128)S(1)} %get-tuple-element.26), channel_id=1, source_target_pairs={{0,1},{1,0},{2,3},{3,2},{4,5},{5,4},{6,7},{7,6},{8,9},{9,8},{10,11... | collective-permute-start | bytes 786440 | tf_op jit(solution)/shard_map/ppermute | solution.py:275
  8.6 6.5 %collective-permute-start.1 = (f32[512,256]{1,0:T(8,128)S(1)}, f32[512,256]{1,0:T(8,128)S(1)}, u32[]{:S(2)}, u32[]{:S(2)}) collective-permute-start(f32[512,256]{1,0:T(8,128)S(1)} %get-tuple-element.27), channel_id=1, source_target_pairs={{0,1},{1,0},{2,3},{3,2},{4,5},{5,4},{6,7},{7,6},{8,9},{9,8},{10,11... | collective-permute-start | bytes 1572872 | tf_op jit(solution)/shard_map/ppermute | solution.py:281
  8.7 6.2 %collective-permute-start.5 = (f32[256,256]{1,0:T(8,128)S(1)}, f32[256,256]{1,0:T(8,128)S(1)}, u32[]{:S(2)}, u32[]{:S(2)}) collective-permute-start(f32[256,256]{1,0:T(8,128)S(1)} %get-tuple-element.37), channel_id=1, source_target_pairs={{0,1},{1,0},{2,3},{3,2},{4,5},{5,4},{6,7},{7,6},{8,9},{9,8},{10,11... | collective-permute-start | bytes 786440 | tf_op jit(solution)/shard_map/ppermute | solution.py:275
  9.1 10.3 %collective-permute-start.2 = (f32[256,256]{1,0:T(8,128)S(1)}, f32[256,256]{1,0:T(8,128)S(1)}, u32[]{:S(2)}, u32[]{:S(2)}) collective-permute-start(f32[256,256]{1,0:T(8,128)S(1)} %add.34), channel_id=1, source_target_pairs={{0,2},{2,4},{4,6},{6,8},{8,10},{10,12},{12,14},{14,0},{1,15},{3,1}... | collective-permute-start | bytes 786440 | tf_op jit(solution)/shard_map/ppermute | solution.py:271
  11.1 8.5 %collective-permute-start.4 = (f32[512,256]{1,0:T(8,128)S(1)}, f32[512,256]{1,0:T(8,128)S(1)}, u32[]{:S(2)}, u32[]{:S(2)}) collective-permute-start(f32[512,256]{1,0:T(8,128)S(1)} %get-tuple-element.35), channel_id=1, source_target_pairs={{0,1},{1,0},{2,3},{3,2},{4,5},{5,4},{6,7},{7,6},{8,9},{9,8},{10,11... | collective-permute-start | bytes 1572872 | tf_op jit(solution)/shard_map/ppermute | solution.py:281
  14.9 7.9 %copy-start = (s32[2,256]{1,0:T(2,128)S(1)}, s32[2,256]{1,0:T(2,128)}, u32[]{:S(2)}) copy-start(s32[2,256]{1,0:T(2,128)} %level_ref.1) | copy-start | bytes 6148
  14.9 7.9 %copy-start.1 = (s32[2]{0:T(128)S(1)}, s32[2]{0:T(128)}, u32[]{:S(2)}) copy-start(s32[2]{0:T(128)} %count_ref.1) | copy-start | bytes 28
  15.0 7.7 %collective-permute-start.6 = (f32[256,256]{1,0:T(8,128)S(1)}, f32[256,256]{1,0:T(8,128)S(1)}, u32[]{:S(2)}, u32[]{:S(2)}) collective-permute-start(f32[256,256]{1,0:T(8,128)S(1)} %add.38), channel_id=1, source_target_pairs={{0,2},{2,4},{4,6},{6,8},{8,10},{10,12},{12,14},{14,0},{1,15},{3,1}... | collective-permute-start | bytes 786440 | tf_op jit(solution)/shard_map/ppermute | solution.py:271
  19.5 10.5 %collective-permute-start.3 = (f32[512,256]{1,0:T(8,128)S(1)}, f32[512,256]{1,0:T(8,128)S(1)}, u32[]{:S(2)}, u32[]{:S(2)}) collective-permute-start(f32[512,256]{1,0:T(8,128)S(1)} %pad_maximum_fusion), channel_id=1, source_target_pairs={{0,2},{2,4},{4,6},{6,8},{8,10},{10,12},{12,14},{14,0},{1,15},{3,1}... | collective-permute-start | bytes 1572872 | tf_op jit(solution)/shard_map/ppermute | solution.py:271
  22.7 12.9 %collective-permute-start.7 = (f32[512,256]{1,0:T(8,128)S(1)}, f32[512,256]{1,0:T(8,128)S(1)}, u32[]{:S(2)}, u32[]{:S(2)}) collective-permute-start(f32[512,256]{1,0:T(8,128)S(1)} %pad_maximum_fusion.1), channel_id=1, source_target_pairs={{0,2},{2,4},{4,6},{6,8},{8,10},{10,12},{12,14},{14,0},{1,15},{3,1}... | collective-permute-start | bytes 1572872 | tf_op jit(solution)/shard_map/ppermute | solution.py:271
  30.1 5.7 %collective-permute-start.9 = (f32[512,256]{1,0:T(8,128)S(1)}, f32[512,256]{1,0:T(8,128)S(1)}, u32[]{:S(2)}, u32[]{:S(2)}) collective-permute-start(f32[512,256]{1,0:T(8,128)S(1)} %add.42.mine_ref), channel_id=1, source_target_pairs={{0,1},{1,0},{2,3},{3,2},{4,5},{5,4},{6,7},{7,6},{8,9},{9,8},{10,11... | collective-permute-start | bytes 1572872 | tf_op jit(solution)/shard_map/ppermute | solution.py:287
  35.7 2.0 %collective-permute-start.8 = (f32[512,256]{1,0:T(8,128)S(1)}, f32[512,256]{1,0:T(8,128)S(1)}, u32[]{:S(2)}, u32[]{:S(2)}) collective-permute-start(f32[512,256]{1,0:T(8,128)S(1)} %add.41.mine_ref), channel_id=1, source_target_pairs={{0,1},{1,0},{2,3},{3,2},{4,5},{5,4},{6,7},{7,6},{8,9},{9,8},{10,11... | collective-permute-start | bytes 1572872 | tf_op jit(solution)/shard_map/ppermute | solution.py:287
